TPU v7x, 128 devices: a whole 4x4x4 slice. The times are simulated.
128 devices in a mesh: rows: 32 (over z, x_hi, y), inst: 4 (over x_lo, core).
Axes of the slice: x: 4 (x_hi: 2, x_lo: 2; x = x_hi * 2 + x_lo), y: 4, z: 4, core: 2. Of those that a mesh axis runs over, the one named last changes fastest.
Arguments:
- adjoint: float32 [8, 5, 589824], P('inst', None, 'rows'), may hold values from -6 to 6
- jacobian: bfloat16 [8, 5, 5, 589824], P('inst', None, None, 'rows'), may hold values from -3 to 3
- source_term: float32 [8, 5, 589824], P('inst', None, 'rows'), may hold values from -6 to 6
- face_area: float32 [131072], P('rows'), may hold values from 0.5 to 8
- face_band: int32 [131072], P('rows'), may hold values from 0 to 199, as said below
- partition_row: int32 [32], P('rows'), may hold values from 0 to 4, as said below
Outputs:
- updated: float32 [8, 5, 589824], P('inst', None, 'rows')
Inputs may be any that keep to these rules, and one draw needn't show every extreme that they name: `face_band`: each half of a partition's face slots names every band of its plane at least once. `partition_row`: every blade row 0 .. 4 owns at least one partition.
All inputs are finite; a program needn't handle non-finite values.
Results may differ from a plain program's by a relative error of at most 0.0003.
Values sent between devices are 32-bit elements; how exact they have to be, the bound alone decides.
A program may use at most 128 MiB of HBM per device.

v0:
```python
import math

import jax
import jax.numpy as jnp
from jax import lax
from jax.sharding import PartitionSpec as P

NT = 8
NV = 5
NB = 200
PLANES = 4
PB = 800


frequency = 1.0
coupling_gain = 2.0
pseudo_step = 0.5


def spectral_matrix():
    index = jnp.arange(NT)
    offset_int = index[:, None] - index[None, :]
    offset = offset_int.astype(jnp.float32)
    safe = jnp.where(offset_int == 0, 1.0, offset)
    parity = jnp.where(jnp.abs(offset_int) % 2 == 0, 1.0, -1.0)
    return jnp.where(offset_int == 0, 0.0, 0.5 * parity / jnp.tan(math.pi * safe / NT))


def shards(adjoint, jacobian, source_term, face_area, face_band, partition_row):
    inst_local = adjoint.shape[0]
    cell_count = adjoint.shape[2]
    face_count = face_area.shape[0]
    matrix = spectral_matrix()
    flux = jnp.sum(jacobian.astype(jnp.float32) * adjoint[:, :, None, :], axis=1)
    my_first = lax.axis_index("inst") * inst_local
    columns = lax.dynamic_slice_in_dim(matrix, my_first, inst_local, 1)
    summed = jnp.einsum(
        "st,svc->tvc",
        columns,
        lax.all_gather(adjoint, "inst", axis=0, tiled=True),
        precision=lax.Precision.HIGHEST,
    )
    coupled = frequency * summed
    owner = partition_row[0]
    position = jnp.arange(face_count)
    plane = jnp.where(
        position < face_count // 2, jnp.maximum(owner - 1, 0), jnp.minimum(owner, PLANES - 1)
    )
    identity = plane * NB + face_band
    table = (identity[:, None] == jnp.arange(PB)[None, :]).astype(jnp.float32)
    face_values = adjoint[:, :, cell_count - face_count :].reshape(inst_local * NV, face_count)
    partial_value = jnp.dot(
        face_values * face_area[None, :], table, precision=lax.Precision.HIGHEST
    )
    weight = jnp.dot(face_area, table, precision=lax.Precision.HIGHEST)
    owned_sum, owned_weight = (
        lax.psum_scatter(partial_value, "rows", scatter_dimension=1, tiled=True),
        lax.psum_scatter(weight, "rows", scatter_dimension=0, tiled=True),
    )
    means = lax.all_gather(owned_sum / owned_weight[None, :], "rows", axis=1, tiled=True)
    face_mean = jnp.dot(means, table.T, precision=lax.Precision.HIGHEST)
    mixing = (coupling_gain * (face_mean - face_values)).reshape(inst_local, NV, face_count)
    residual = flux + coupled - source_term
    residual = jnp.concatenate(
        [
            residual[:, :, : cell_count - face_count],
            residual[:, :, cell_count - face_count :] + mixing,
        ],
        axis=2,
    )
    return adjoint - pseudo_step * residual


def solution(mesh):
    placed = (
        P("inst", None, "rows"),
        P("inst", None, None, "rows"),
        P("inst", None, "rows"),
        P("rows"),
        P("rows"),
        P("rows"),
    )
    return jax.shard_map(
        shards, mesh=mesh, in_specs=placed, out_specs=P("inst", None, "rows"), check_vma=False
    )
```

profile of v0, /device:TPU:0, one launch (start us, length us, event | category | flops | bytes accessed | tf_op | source)
XLA Modules:
  0.0 321.4 jit_solution(6628498493089733138)
XLA Ops:
  6.5 0.0 copy-start.5
  6.5 0.0 copy-start.3
  6.5 0.0 copy-start.4
  6.5 0.0 all-gather.3.cloned.1.call-start
  6.5 2.7 copy.16
  9.2 0.0 all-gather.3.cloned.1.call-update
  9.2 0.9 slice.11
  10.8 0.1 copy.18
  11.0 0.0 copy-done.5
  11.0 0.6 dynamic-slice
  12.3 0.0 copy-done.3
  12.3 0.0 copy-done.4
  12.3 5.8 %fusion.10 = f32[800]{0:T(1024)S(1)} fusion(f32[4096,1]{0,1:T(1,128)S(1)} %bitcast.17, s32[4096]{0:T(1024)S(1)} %multiply_add_fusion), kind=kOutput, calls=%fused_computation.13 | convolution fusion | flops 42598400 | bytes 35968 | tf_op jit(solution)/shard_map/dot_general | solution.py:55
  18.1 0.0 copy-start
  18.1 0.0 copy-start.1
  18.1 5.8 %fusion.3 = f32[10,800]{1,0:T(8,128)S(1)} fusion(s32[4096]{0:T(1024)S(1)} %multiply_add_fusion, f32[10,4096]{1,0:T(8,128)S(1)} %reshape.16, f32[4096]{0:T(1024)S(1)} %copy-done.4), kind=kOutput, calls=%fused_computation.5 | convolution fusion | flops 396533760 | bytes 228608 | tf_op jit(solution)/shard_map/dot_general | solution.py:52
  23.9 185.6 %all-reduce.2 = (f32[10,800]{1,0:T(8,128)S(1)}, f32[800]{0:T(1024)S(1)}) all-reduce(f32[10,800]{1,0:T(8,128)S(1)} %fusion.3, f32[800]{0:T(1024)S(1)} %fusion.10), channel_id=2, replica_groups=mesh['rows'=32,'inst'=4] {'rows'}, use_global_device_ids=true, to_apply=%region_1.2.clone | all-reduce | flops 8800 | bytes 70400
  209.4 0.1 dynamic-slice.3
  209.5 0.1 fusion.14
  209.6 88.8 %all-gather = f32[32,25,10]{1,2,0:T(8,128)S(1)} all-gather(f32[1,25,10]{1,2,0:T(8,128)S(1)} %fusion.14), channel_id=1, replica_groups=mesh['rows'=32,'inst'=4] {'rows'}, dimensions={0}, use_global_device_ids=true | all-gather | bytes 33000 | tf_op jit(solution)/shard_map/all_gather | solution.py:60
  298.4 0.1 copy.19
  298.5 0.1 reshape.19
  298.6 4.3 %fusion.8 = f32[10,4096]{1,0:T(8,128)S(1)} fusion(f32[10,4096]{1,0:T(8,128)S(1)} %reshape.16, f32[800,10]{0,1:T(8,128)S(1)} %reshape.19, s32[4096]{0:T(1024)S(1)} %multiply_add_fusion), kind=kOutput, calls=%fused_computation.10 | convolution fusion | flops 396574720 | bytes 376064 | tf_op jit(solution)/shard_map/dot_general | solution.py:61
  302.9 0.7 reshape.17
  303.6 0.1 divide_select_fusion
  303.7 0.0 copy-done
  303.7 0.0 copy-done.1
  303.7 2.2 multiply_reduce_fusion
  305.9 0.0 copy-start.2
  305.9 0.0 all-gather.3.cloned.1.call-done
  305.9 6.9 %fusion = f32[2,5,18432]{2,0,1:T(2,128)S(1)} fusion(f32[2,5,18432]{2,0,1:T(2,128)} %param.8, f32[2,5,18432]{2,0,1:T(2,128)S(1)} %multiply_reduce_fusion, f32[8,5,18432]{2,1,0:T(8,128)} %all-gather.3.cloned.1.call-done, f32[8,8]{0,1:T(8,128)S(1)} %divide_select_fusion, s32[]{:T(128)S(6)} %select_n.29), kind=kOutput, calls=%fused_computation.1 | convolution fusion | flops 18063360 | bytes 5161988 | tf_op jit(solution)/shard_map/st,svc->tvc/dot_general | solution.py:37
  312.9 0.0 copy-done.2
  313.0 0.2 slice_add_fusion
  313.1 1.4 fusion.11
  (3 shorter events, 0.1 us)
Async XLA Ops:
  6.5 4.5 %copy-start.5 = (u32[128]{0:T(128)S(1)}, u32[128]{0:T(128)}, u32[]{:S(2)}) copy-start(u32[128]{0:T(128)} %constant.58) | copy-start | bytes 1540
  6.5 5.7 %copy-start.3 = (s32[4096]{0:T(1024)S(1)}, s32[4096]{0:T(1024)}, u32[]{:S(2)}) copy-start(s32[4096]{0:T(1024)} %param.10) | copy-start | bytes 49156
  6.5 5.7 %copy-start.4 = (f32[4096]{0:T(1024)S(1)}, f32[4096]{0:T(1024)}, u32[]{:S(2)}) copy-start(f32[4096]{0:T(1024)} %param.9) | copy-start | bytes 49156
  6.5 299.4 %all-gather.3.cloned.1.call-start = ((), (), s32[]{:S(2)}) async-start(), calls=%async_computation | async-start | bytes 5898240 | tf_op jit(solution)/shard_map/all_gather | solution.py:40
  18.1 285.6 %copy-start = (f32[2,5,18432]{2,0,1:T(2,128)S(1)}, f32[2,5,18432]{2,0,1:T(2,128)}, u32[]{:S(2)}) copy-start(f32[2,5,18432]{2,0,1:T(2,128)} %param.6) | copy-start | bytes 2211844
  18.1 285.6 %copy-start.1 = (bf16[2,5,5,18432]{3,0,2,1:T(2,128)(2,1)S(1)}, bf16[2,5,5,18432]{3,0,2,1:T(2,128)(2,1)}, u32[]{:S(2)}) copy-start(bf16[2,5,5,18432]{3,0,2,1:T(2,128)(2,1)} %param.7) | copy-start | bytes 5529604
  305.9 7.0 %copy-start.2 = (f32[2,5,4096]{2,1,0:T(8,128)S(1)}, f32[2,5,4096]{2,1,0:T(8,128)}, u32[]{:S(2)}) copy-start(f32[2,5,4096]{2,1,0:T(8,128)} %reshape.17) | copy-start | bytes 491524
Sparse Core Ops, SparseCore 0:
  9.4 53.2 all-gather.2
where the time goes:
time: 322 us; the launch traced here: 321 us
  blocking collectives  274 us (85%)
  matrix products  22.8 us (7%)
  between operations  14.8 us (5%)
  local copies, waits for them, and re-layouts  5.43 us (2%)
  other arithmetic  3.9 us (1%)
    unnamed x1, blocking collectives  186 us
    all_gather x1, blocking collectives, shards(): lax.all_gather(owned_sum / owned_weight[None, :], 'rows', axis=1, tiled=T...  88.8 us
    dot_general x1, matrix products, shards(): jnp.einsum('st,svc->tvc', columns, lax.all_gather(adjoint, 'inst', axis=0...  6.94 us
  transfers between devices with their start and end apart: 1, of which 0 were waited for; matrix products, arithmetic and copies ran while one was open for 6% of the time, Pallas kernels for 0%

commit v1 on v0

v1 whole, which is shorter than its diff:
```python
import jax
import jax.numpy as jnp
import numpy as np
from jax import lax
from jax.experimental import pallas as pl
from jax.experimental.pallas import tpu as pltpu
from jax.sharding import PartitionSpec as P

MESH = pl.DeviceIdType.MESH
NT = 8
NV = 5
NB = 200
PLANES = 4
BANDS = 256
LANES = 128

frequency = 1.0
coupling_gain = 2.0
pseudo_step = 0.5

GROUP = 4
CHUNKS = 9
RAW = 1
OWNERS = 16


def spectral(offset):
    if offset % NT == 0:
        return 0.0
    angle = np.float32(np.pi * offset / NT)
    return float(np.float32(0.5 * (-1) ** (offset % 2)) / np.tan(angle))


def weight_of(offset):
    return -pseudo_step * frequency * spectral(offset)


def pick(first, up, down):
    return jnp.where(first, jnp.float32(up), jnp.float32(down))


def swap(x):
    even = lax.broadcasted_iota(jnp.int32, x.shape, x.ndim - 2) % 2 == 0
    return jnp.where(even, pltpu.roll(x, 7, x.ndim - 2), pltpu.roll(x, 1, x.ndim - 2))


def split(x):
    high = x.astype(jnp.bfloat16)
    low = (x - high.astype(jnp.float32)).astype(jnp.bfloat16)
    return jnp.concatenate([high, low], axis=0)


def kernel(
    adjoint, jacobian, source, area, band, owner, updated,
    own, jac, src, sibling, result, outbox, inbox, relay, area_v, band_v,
    table, weighted, part, gathered, half_sum, other_sum, totals,
    local_sem, result_sem, sib_send, sib_recv, link_send, link_recv, relay_send, relay_recv,
    rs_send, rs_recv, x_send, x_recv, ag_send, ag_recv,
):
    rows, inst = lax.axis_index("rows"), lax.axis_index("inst")
    z, x_hi, y = rows // 8, (rows // 4) % 2, rows % 4
    first_core = inst % 2 == 0
    sibling_id = (rows, inst + 1 - 2 * (inst % 2))
    link_id = (rows, (inst + 2) % 4)
    across_id = (z * 8 + (1 - x_hi) * 4 + y, inst)
    me = z * 4 + y
    faces = weighted.shape[1]
    half = faces // 2
    face_groups = faces // (4 * LANES)
    face_start = GROUP * CHUNKS - face_groups

    def place(k):
        return (z + k // 4) % 4, (y + k % 4) % 4

    def device(k):
        zd, yd = place(k)
        return (zd * 8 + x_hi * 4 + yd, inst)

    def span(c):
        return pl.ds(c * GROUP, GROUP)

    def each(low, high, act):
        def body(k, carry):
            act(k)
            return carry

        lax.fori_loop(low, high, body, 0)

    def fetch(k, a, b):
        copy = pltpu.make_async_copy(a, b, local_sem.at[k])
        copy.start()
        return copy

    got_area = fetch(0, area, area_v)
    got_band = fetch(1, band, band_v)
    tail, front = pl.ds(face_start, face_groups), pl.ds(0, face_start)
    got_faces = fetch(3, adjoint.at[:, tail], own.at[:, tail])
    got_front = fetch(4, adjoint.at[:, front], own.at[:, front])
    got_jac = fetch(5, jacobian, jac)
    got_src = fetch(6, source, src)

    barrier = pltpu.get_barrier_semaphore()

    def announce(device_id):
        pl.semaphore_signal(barrier, inc=1, device_id=device_id, device_id_type=MESH)

    for partner in (sibling_id, link_id, across_id):
        announce(partner)
    each(1, OWNERS, lambda k: announce(device(k)))

    got_area.wait()
    got_band.wait()
    got_faces.wait()
    band_index = lax.broadcasted_iota(jnp.int32, (BANDS, LANES), 0)
    weighted[...] = jnp.zeros_like(weighted)

    def weigh(g):
        for r in range(4):
            tile = 4 * g + r
            here = pl.ds(pl.multiple_of(tile * LANES, LANES), LANES)
            size = area_v[pl.ds(tile, 1), :]
            for v in range(NV):
                weighted[2 * v : 2 * v + 2, here] = own[v, face_start + g, 2 * r : 2 * r + 2, :] * size
            weighted[2 * NV : 2 * NV + 1, here] = size
            table[:, here] = jnp.where(band_index == band_v[pl.ds(tile, 1), :], 1.0, 0.0).astype(jnp.bfloat16)

    each(0, face_groups, weigh)

    row = owner[0]
    planes = (jnp.maximum(row - 1, 0), jnp.minimum(row, PLANES - 1))
    on_plane = [
        [jnp.where(planes[h] == p, jnp.float32(1), jnp.float32(0)) for p in range(PLANES)]
        for h in range(2)
    ]
    sums = []
    for h in range(2):
        cut = slice(h * half, (h + 1) * half)
        both = lax.dot_general(
            split(weighted[:, cut]), table[:, cut], (((1,), (1,)), ((), ())),
            preferred_element_type=jnp.float32,
        )
        sums.append(both[0:16] + both[16:32])
    for p in range(PLANES):
        here = sums[0] * on_plane[0][p] + sums[1] * on_plane[1][p]
        for q in range(4):
            part[4 * p + q] = here[8 * (q // 2) : 8 * (q // 2) + 8, LANES * (q % 2) : LANES * (q % 2 + 1)]

    pl.semaphore_wait(barrier, OWNERS + 2)

    def remote(a, b, send, recv, device_id):
        return pltpu.make_async_remote_copy(
            a, b, send, recv, device_id=device_id, device_id_type=MESH
        )

    def raw_to_link(c):
        return remote(own.at[:, span(c)], inbox.at[:, span(c)], link_send.at[c], link_recv.at[c], link_id)

    def to_link(c):
        return remote(outbox.at[:, span(c)], inbox.at[:, span(c)], link_send.at[c], link_recv.at[c], link_id)

    def to_sibling(c):
        return remote(own.at[:, span(c)], sibling.at[:, span(c)], sib_send.at[c], sib_recv.at[c], sibling_id)

    def to_relay(c):
        return remote(inbox.at[:, span(c)], relay.at[:, span(c)], relay_send.at[c], relay_recv.at[c], sibling_id)

    def scatter(k):
        zd, yd = place(k)
        return remote(part.at[zd * 4 + yd], gathered.at[k], rs_send.at[k], rs_recv.at[k], device(k))

    def gather(k):
        return remote(totals.at[me], totals.at[me], ag_send.at[k], ag_recv.at[k], device(k))

    across = remote(half_sum, other_sum, x_send, x_recv, across_id)

    got_front.wait()
    each(0, RAW, lambda c: raw_to_link(c).start())
    each(1, OWNERS, lambda k: scatter(k).start())
    each(0, CHUNKS, lambda c: to_sibling(c).start())

    odd = lax.broadcasted_iota(jnp.int32, (8, LANES), 0) % 2 == 1

    def weights(by_offset):
        return by_offset[0], jnp.where(odd, by_offset[1], by_offset[-1])

    shifts = (-1, 0, 1)
    inner = weights({d: weight_of(d) for d in shifts})
    facing = weights({d: weight_of(4 + d) for d in shifts})
    near = weights({d: pick(first_core, weight_of(2 + d), weight_of(-2 + d)) for d in shifts})
    away = weights({d: pick(first_core, weight_of(-2 + d), weight_of(2 + d)) for d in shifts})

    def combine(a, b, wa, wb):
        return wa[0] * a + wb[0] * b + swap(wa[1] * a + wb[1] * b)

    def send_partial(c):
        to_sibling(c).wait_recv()
        for v in range(NV):
            outbox[v, span(c)] = combine(own[v, span(c)], sibling[v, span(c)], facing, away)
        to_link(c).start()

    each(0, RAW, lambda c: to_sibling(c).wait_recv())
    each(RAW, CHUNKS, send_partial)

    got_jac.wait()
    got_src.wait()

    def base(c):
        here = span(c)
        half_groups = pl.ds(c * (GROUP // 2), GROUP // 2)
        state = [own[w, here] for w in range(NV)]
        for v in range(NV):
            flux = 0.0
            for w in range(NV):
                block = jac[w, v, half_groups].astype(jnp.float32).reshape(GROUP, 8, LANES)
                flux = flux + block * state[w]
            coupled = combine(state[v], sibling[v, here], inner, near)
            result[v, here] = state[v] + coupled - pseudo_step * (flux - src[v, here])

    each(0, CHUNKS, base)

    each(1, OWNERS, lambda k: scatter(k).wait())
    total = part[me]
    for k in range(1, OWNERS):
        total = total + gathered[k]
    half_sum[...] = total
    across.start()

    def pass_on(c):
        raw_to_link(c).wait_recv()
        to_relay(c).start()

    each(0, RAW, pass_on)

    across.wait()
    totals[me] = half_sum[...] + other_sum[...]
    each(1, OWNERS, lambda k: gather(k).start())

    def to_result(c):
        return pltpu.make_async_copy(result.at[:, span(c)], updated.at[:, span(c)], result_sem.at[c])

    def finish_raw(c):
        to_relay(c).wait()
        for v in range(NV):
            result[v, span(c)] += combine(inbox[v, span(c)], relay[v, span(c)], facing, away)
        to_result(c).start()

    each(0, RAW, finish_raw)

    def finish(c):
        to_link(c).wait_recv()
        result[:, span(c)] += inbox[:, span(c)]
        to_result(c).start()

    each(RAW, face_start // GROUP, finish)

    each(1, OWNERS, lambda k: gather(k).wait())
    for h in range(2):
        top, bottom = 0.0, 0.0
        for p in range(PLANES):
            tile = [totals[4 * p + q] for q in range(4)]
            top = top + jnp.concatenate(tile[0:2], axis=1) * on_plane[h][p]
            bottom = bottom + jnp.concatenate(tile[2:4], axis=1) * on_plane[h][p]
        total_area = bottom[2:3]
        total_area = jnp.where(total_area > 0, total_area, 1.0)
        means = split(jnp.concatenate([top / total_area, bottom / total_area], axis=0))
        cut = slice(h * half, (h + 1) * half)
        both = jnp.dot(means, table[:, cut], preferred_element_type=jnp.float32)
        weighted[:, cut] = (both[0:16] + both[16:32]) * (pseudo_step * coupling_gain)

    def mix(g):
        here = face_start + g
        for v in range(NV):
            result[v, here] += own[v, here] * (pseudo_step * coupling_gain)
            for r in range(4):
                lanes = pl.ds(pl.multiple_of((4 * g + r) * LANES, LANES), LANES)
                result[v, here, 2 * r : 2 * r + 2, :] -= weighted[2 * v : 2 * v + 2, lanes]

    each(0, face_groups, mix)
    each(face_start // GROUP, CHUNKS, finish)

    each(0, CHUNKS, lambda c: to_result(c).wait())
    each(0, CHUNKS, lambda c: to_sibling(c).wait_send())
    each(0, RAW, lambda c: raw_to_link(c).wait_send())
    each(RAW, CHUNKS, lambda c: to_link(c).wait_send())


def fold(x):
    cells = x.shape[2]
    x = x.reshape(2, NV, cells // (4 * LANES), 4, LANES).transpose(1, 2, 3, 0, 4)
    return x.reshape(NV, cells // (4 * LANES), 8, LANES)


def unfold(x):
    x = x.reshape(NV, x.shape[1], 4, 2, LANES).transpose(3, 0, 1, 2, 4)
    return x.reshape(2, NV, -1)


def fold_jacobian(x):
    cells = x.shape[3]
    x = x.reshape(2, NV, NV, cells // (8 * LANES), 8, LANES).transpose(1, 2, 3, 4, 0, 5)
    return x.reshape(NV, NV, cells // (8 * LANES), 16, LANES)


def shards(adjoint, jacobian, source_term, face_area, face_band, partition_row):
    cells, faces = adjoint.shape[2], face_area.shape[0]
    groups = cells // (4 * LANES)
    assert groups == GROUP * CHUNKS
    f32, bf16, i32 = jnp.float32, jnp.bfloat16, jnp.int32
    dma = pltpu.SemaphoreType.DMA
    state = pltpu.VMEM((NV, groups, 8, LANES), f32)
    tile = pltpu.VMEM((8, LANES), f32)
    tiles = pltpu.VMEM((OWNERS, 8, LANES), f32)
    updated = pl.pallas_call(
        kernel,
        out_shape=jax.ShapeDtypeStruct((NV, groups, 8, LANES), f32),
        in_specs=[pl.BlockSpec(memory_space=pl.ANY)] * 5 + [pl.BlockSpec(memory_space=pltpu.SMEM)],
        out_specs=pl.BlockSpec(memory_space=pl.ANY),
        scratch_shapes=[
            state,
            pltpu.VMEM((NV, NV, groups // 2, 16, LANES), bf16),
            state,
            state,
            state,
            state,
            state,
            pltpu.VMEM((NV, RAW * GROUP, 8, LANES), f32),
            pltpu.VMEM((faces // LANES, LANES), f32),
            pltpu.VMEM((faces // LANES, LANES), i32),
            pltpu.VMEM((BANDS, faces), bf16),
            pltpu.VMEM((16, faces), f32),
            tiles,
            tiles,
            tile,
            tile,
            tiles,
            dma((7,)),
            dma((CHUNKS,)),
            dma((CHUNKS,)),
            dma((CHUNKS,)),
            dma((CHUNKS,)),
            dma((CHUNKS,)),
            dma((RAW,)),
            dma((RAW,)),
            dma((OWNERS,)),
            dma((OWNERS,)),
            dma,
            dma,
            dma((OWNERS,)),
            dma((OWNERS,)),
        ],
        compiler_params=pltpu.CompilerParams(
            collective_id=0, has_side_effects=True, vmem_limit_bytes=60 << 20
        ),
    )(
        fold(adjoint),
        fold_jacobian(jacobian),
        fold(source_term),
        face_area.reshape(faces // LANES, LANES),
        face_band.reshape(faces // LANES, LANES),
        partition_row,
    )
    return unfold(updated)


def solution(mesh):
    placed = (
        P("inst", None, "rows"),
        P("inst", None, None, "rows"),
        P("inst", None, "rows"),
        P("rows"),
        P("rows"),
        P("rows"),
    )
    return jax.shard_map(
        shards, mesh=mesh, in_specs=placed, out_specs=P("inst", None, "rows"), check_vma=False
    )
```

time: 322 us -> 36.2 us (0.11)
  blocking collectives: 274 us -> 0 us
  Pallas kernels: 0 us -> 33.3 us
  matrix products: 22.8 us -> 0 us
  between operations: 14.8 us -> 0.66 us
  other arithmetic: 3.9 us -> 0 us
  local copies, waits for them, and re-layouts: 5.43 us -> 2.03 us
    unnamed x1 -> x0, blocking collectives: 186 us -> none
    all_gather x1 -> x0, blocking collectives: 88.8 us -> none  [shards(): lax.all_gather(owned_sum / owned_weight[None, :], 'rows', axis=1, tiled=T...]
    pallas_call x0 -> x1, Pallas kernels: none -> 33.3 us  [shards(): pl.pallas_call(kernel, out_shape=jax.ShapeDtypeStruct((NV, groups, 8, LAN...]
    dot_general x4 -> x0, matrix products: 22.8 us -> none  [the longest x1 6.94 us: shards(): jnp.einsum('st,svc->tvc', columns, lax.all_gather(adjoint, 'inst', axis=0...]
  transfers between devices with their start and end apart: 1 -> 0, of which waited for: 0 -> 0; matrix products, arithmetic and copies ran while one was open for 6% -> 0% of each run, Pallas kernels for 0% -> 0%
where the time goes in v1:
time: 36.2 us; the launch traced here: 35.9 us
  Pallas kernels  33.3 us (92%)
  local copies, waits for them, and re-layouts  2.03 us (6%)
  between operations  0.66 us (2%)
    pallas_call x1, Pallas kernels, shards(): pl.pallas_call(kernel, out_shape=jax.ShapeDtypeStruct((NV, groups, 8, LAN...  33.3 us
    unnamed x1, local copies, waits for them, and re-layouts  2.03 us

profile of v1, /device:TPU:0, one launch (start us, length us, event | category | flops | bytes accessed | tf_op | source)
XLA Modules:
  0.0 35.9 jit_solution(9929362425756960881)
XLA Ops:
  0.7 33.3 %shard_map.64 = f32[5,36,8,128]{3,2,1,0:T(8,128)} custom-call(f32[5,36,8,128]{3,2,1,0:T(8,128)} %bitcast.24, bf16[5,5,18,16,128]{4,3,2,1,0:T(8,128)(2,1)} %bitcast.23, f32[5,36,8,128]{3,2,1,0:T(8,128)} %bitcast.25, f32[32,128]{1,0:T(8,128)} %bitcast.26, s32[32,128]{1,0:T(8,128)} %bitcast.27, s32[1]{0:T(128)S(6)} %copy.12.owner), custom_call_target="tpu_custom_call" | custom-call | tf_op jit(solution)/shard_map/pallas_call | solution.py:313
  33.9 2.0 %copy.13 = f32[2,5,18432]{2,0,1:T(2,128)} copy(f32[2,5,18432]{2,0,1:T(2,128)} %bitcast.22) | data formatting | bytes 1474560

commit v2 on v1

v2 whole, which is shorter than its diff:
```python
import jax
import jax.numpy as jnp
import numpy as np
from jax import lax
from jax.experimental import pallas as pl
from jax.experimental.pallas import tpu as pltpu
from jax.sharding import PartitionSpec as P

MESH = pl.DeviceIdType.MESH
NT = 8
NV = 5
NB = 200
PLANES = 4
BANDS = 256
LANES = 128

frequency = 1.0
coupling_gain = 2.0
pseudo_step = 0.5

GROUP = 4
CHUNKS = 9
RAW = 2
OWNERS = 16


def spectral(offset):
    if offset % NT == 0:
        return 0.0
    angle = np.float32(np.pi * offset / NT)
    return float(np.float32(0.5 * (-1) ** (offset % 2)) / np.tan(angle))


def weight_of(offset):
    return -pseudo_step * frequency * spectral(offset)


def pick(first, up, down):
    return jnp.where(first, jnp.float32(up), jnp.float32(down))


def swap(x):
    even = lax.broadcasted_iota(jnp.int32, x.shape, x.ndim - 2) % 2 == 0
    return jnp.where(even, pltpu.roll(x, 7, x.ndim - 2), pltpu.roll(x, 1, x.ndim - 2))


def split(x):
    high = x.astype(jnp.bfloat16)
    low = (x - high.astype(jnp.float32)).astype(jnp.bfloat16)
    return jnp.concatenate([high, low], axis=0)


def kernel(
    adjoint, jacobian, source, area, band, owner, result,
    own, jac, src, sibling, outbox, inbox, relay, area_v, band_v,
    table, weighted, part, gathered, half_sum, other_sum, total, means,
    near_sem, local_sem, sib_send, sib_recv, link_send, link_recv, relay_send, relay_recv,
    rs_send, rs_recv, x_send, x_recv, ag_send, ag_recv,
):
    rows, inst = lax.axis_index("rows"), lax.axis_index("inst")
    z, x_hi, y = rows // 8, (rows // 4) % 2, rows % 4
    core = inst % 2
    first, second = core == 0, core == 1
    sibling_id = (rows, inst + 1 - 2 * core)
    link_id = (rows, (inst + 2) % 4)
    diagonal_id = (rows, (inst + 2) % 4 + 1 - 2 * core)
    across_id = (z * 8 + (1 - x_hi) * 4 + y, inst)
    me = z * 4 + y
    faces = weighted.shape[1]
    half = faces // 2
    face_groups = faces // (4 * LANES)
    face_start = GROUP * CHUNKS - face_groups
    face_chunk = face_start // GROUP

    def place(k):
        return (z + k // 4) % 4, (y + k % 4) % 4

    def device(k, inst):
        zd, yd = place(k)
        return (zd * 8 + x_hi * 4 + yd, inst)

    def span(c):
        return pl.ds(c * GROUP, GROUP)

    def each(low, high, act):
        def body(k, carry):
            act(k)
            return carry

        lax.fori_loop(low, high, body, 0)

    def fetch(k, a, b):
        copy = pltpu.make_async_copy(a, b, local_sem.at[k])
        copy.start()
        return copy

    def signal(sem, device_id):
        pl.semaphore_signal(sem, inc=1, device_id=device_id, device_id_type=MESH)

    def remote(a, b, send, recv, device_id):
        return pltpu.make_async_remote_copy(
            a, b, send, recv, device_id=device_id, device_id_type=MESH
        )

    def to_sibling(c):
        return remote(
            adjoint.at[:, span(c)], sibling.at[:, span(c)], sib_send.at[c], sib_recv.at[c], sibling_id
        )

    def to_link(source_ref, c, core_there):
        target = (rows, (inst + 2) % 4 + core_there)
        return remote(
            source_ref.at[:, span(c)], inbox.at[:, span(c)], link_send.at[core_there, c], link_recv.at[c], target
        )

    def to_relay(c):
        return remote(inbox.at[:, span(c)], relay.at[:, span(c)], relay_send.at[c], relay_recv.at[c], sibling_id)

    def scatter(k):
        zd, yd = place(k)
        return remote(part.at[zd * 4 + yd], gathered.at[k], rs_send.at[k], rs_recv.at[k], device(k, inst))

    slot = 2 * z + y % 2
    served = inst - y // 2

    def gather(k):
        return remote(total, means.at[slot], ag_send.at[k], ag_recv.at[slot], device(k, served))

    def keep():
        return pltpu.make_async_copy(total, means.at[slot], ag_recv.at[slot])

    def arrived(n):
        return remote(total, means.at[n], ag_send.at[0], ag_recv.at[n], sibling_id)

    across = remote(half_sum, other_sum, x_send, x_recv, across_id)

    barrier = pltpu.get_barrier_semaphore()

    @pl.when(first)
    def _():
        signal(barrier, link_id)

    @pl.when(second)
    def _():
        signal(barrier, sibling_id)
        signal(barrier, diagonal_id)

    tail, front = pl.ds(face_start, face_groups), pl.ds(0, face_start)
    got_faces = fetch(0, adjoint.at[:, tail], own.at[:, tail])
    got_area = fetch(1, area, area_v)
    got_band = fetch(2, band, band_v)
    got_front = fetch(3, adjoint.at[:, front], own.at[:, front])
    got_jac = fetch(4, jacobian, jac)
    got_src = fetch(5, source, src)

    @pl.when(first)
    def _():
        pl.semaphore_wait(barrier, 3)
        signal(near_sem, sibling_id)
        each(0, RAW, lambda c: to_link(adjoint, c, 0).start())
        each(face_chunk, CHUNKS, lambda c: to_sibling(c).start())
        each(0, face_chunk, lambda c: to_sibling(c).start())

    @pl.when(second)
    def _():
        pl.semaphore_wait(near_sem, 1)
        each(1, OWNERS, lambda k: signal(barrier, device(k, inst)))
        signal(barrier, across_id)
        each(0, CHUNKS, lambda c: to_sibling(c).start())

    got_area.wait()
    got_band.wait()
    band_index = lax.broadcasted_iota(jnp.int32, (BANDS, LANES), 0)

    def mark(n):
        here = pl.ds(pl.multiple_of(n * LANES, LANES), LANES)
        table[:, here] = jnp.where(band_index == band_v[pl.ds(n, 1), :], 1.0, 0.0).astype(jnp.bfloat16)

    row = owner[0]
    planes = (jnp.maximum(row - 1, 0), jnp.minimum(row, PLANES - 1))
    on_plane = [
        [jnp.where(planes[h] == p, jnp.float32(1), jnp.float32(0)) for p in range(PLANES)]
        for h in range(2)
    ]

    def weigh(values, top):
        def group(g):
            for r in range(4):
                tile = 4 * g + r
                here = pl.ds(pl.multiple_of(tile * LANES, LANES), LANES)
                size = area_v[pl.ds(tile, 1), :]
                for v in range(NV):
                    weighted[top + 2 * v : top + 2 * v + 2, here] = (
                        values[v, face_start + g, 2 * r : 2 * r + 2, :] * size
                    )
                weighted[top + 2 * NV : top + 2 * NV + 1, here] = size

        each(0, face_groups, group)

    @pl.when(second)
    def _():
        each(0, faces // LANES, mark)
        weighted[...] = jnp.zeros_like(weighted)
        got_faces.wait()
        weigh(own, 0)
        each(face_chunk, CHUNKS, lambda c: to_sibling(c).wait_recv())
        weigh(sibling, 16)
        sums = []
        for h in range(2):
            cut = slice(h * half, (h + 1) * half)
            both = lax.dot_general(
                split(weighted[:, cut]), table[:, cut], (((1,), (1,)), ((), ())),
                preferred_element_type=jnp.float32,
            )
            sums.append(both[0:32] + both[32:64])
        for p in range(PLANES):
            here = sums[0] * on_plane[0][p] + sums[1] * on_plane[1][p]
            for q in range(4):
                part[4 * p + q] = here[
                    16 * (q // 2) : 16 * (q // 2) + 16, LANES * (q % 2) : LANES * (q % 2 + 1)
                ]
        pl.semaphore_wait(barrier, OWNERS)
        each(1, OWNERS, lambda k: scatter(k).start())

    odd = lax.broadcasted_iota(jnp.int32, (8, LANES), 0) % 2 == 1

    def weights(by_offset):
        return by_offset[0], jnp.where(odd, by_offset[1], by_offset[-1])

    shifts = (-1, 0, 1)
    inner = weights({d: weight_of(d) for d in shifts})
    facing = weights({d: weight_of(4 + d) for d in shifts})
    up = weights({d: weight_of(2 + d) for d in shifts})
    down = weights({d: weight_of(-2 + d) for d in shifts})
    near = weights({d: pick(first, weight_of(2 + d), weight_of(-2 + d)) for d in shifts})
    away = weights({d: pick(first, weight_of(-2 + d), weight_of(2 + d)) for d in shifts})

    def combine(a, b, wa, wb):
        return wa[0] * a + wb[0] * b + swap(wa[1] * a + wb[1] * b)

    @pl.when(first)
    def _():
        got_front.wait()
        got_faces.wait()

        def send_raw(c):
            to_sibling(c).wait_recv()
            to_link(sibling, c, 1).start()

        def send_partial(c):
            to_sibling(c).wait_recv()
            for v in range(NV):
                a, b = own[v, span(c)], sibling[v, span(c)]
                outbox[0, v, span(c)] = combine(a, b, facing, down)
                outbox[1, v, span(c)] = combine(b, a, facing, up)
            to_link(outbox.at[0], c, 0).start()
            to_link(outbox.at[1], c, 1).start()

        each(0, RAW, send_raw)
        each(RAW, CHUNKS, send_partial)
        each(0, faces // LANES, mark)

    @pl.when(second)
    def _():
        each(0, face_chunk, lambda c: to_sibling(c).wait_recv())
        got_front.wait()

    got_jac.wait()
    got_src.wait()

    def base(c):
        here = span(c)
        half_groups = pl.ds(c * (GROUP // 2), GROUP // 2)
        state = [own[w, here] for w in range(NV)]
        for v in range(NV):
            flux = 0.0
            for w in range(NV):
                block = jac[w, v, half_groups].astype(jnp.float32).reshape(GROUP, 8, LANES)
                flux = flux + block * state[w]
            coupled = combine(state[v], sibling[v, here], inner, near)
            result[v, here] = state[v] + coupled - pseudo_step * (flux - src[v, here])

    each(0, CHUNKS, base)

    @pl.when(second)
    def _():
        each(1, OWNERS, lambda k: scatter(k).wait())
        sum_here = part[me]
        for k in range(1, OWNERS):
            sum_here = sum_here + gathered[k]
        half_sum[...] = sum_here
        across.start()
        across.wait()
        total[...] = half_sum[...] + other_sum[...]
        each(1, OWNERS, lambda k: gather(k).start())

        @pl.when(y >= 2)
        def _():
            gather(0).start()

        @pl.when(y < 2)
        def _():
            keep().start()

    def pass_on(c):
        to_link(inbox, c, 0).wait_recv()
        to_relay(c).start()

    each(0, RAW, pass_on)

    def finish_raw(c):
        to_relay(c).wait()
        for v in range(NV):
            result[v, span(c)] += combine(inbox[v, span(c)], relay[v, span(c)], facing, away)

    each(0, RAW, finish_raw)

    def finish(c):
        to_link(inbox, c, 0).wait_recv()
        result[:, span(c)] += inbox[:, span(c)]

    each(RAW, face_chunk, finish)

    each(0, OWNERS // 2, lambda n: arrived(n).wait_recv())
    for h in range(2):
        table_sum = 0.0
        for p in range(PLANES):
            table_sum += jnp.concatenate([means[2 * p], means[2 * p + 1]], axis=1) * on_plane[h][p]
        total_area = table_sum[2 * NV : 2 * NV + 1]
        total_area = jnp.where(total_area > 0, total_area, 1.0)
        cut = slice(h * half, (h + 1) * half)
        both = jnp.dot(split(table_sum / total_area), table[:, cut], preferred_element_type=jnp.float32)
        weighted[0:16, cut] = (both[0:16] + both[16:32]) * (pseudo_step * coupling_gain)

    def mix(g):
        here = face_start + g
        for v in range(NV):
            result[v, here] += own[v, here] * (pseudo_step * coupling_gain)
            for r in range(4):
                lanes = pl.ds(pl.multiple_of((4 * g + r) * LANES, LANES), LANES)
                result[v, here, 2 * r : 2 * r + 2, :] -= weighted[2 * v : 2 * v + 2, lanes]

    each(0, face_groups, mix)
    each(face_chunk, CHUNKS, finish)

    each(0, CHUNKS, lambda c: to_sibling(c).wait_send())

    @pl.when(first)
    def _():
        each(0, CHUNKS, lambda c: to_link(inbox, c, 0).wait_send())
        each(0, CHUNKS, lambda c: to_link(inbox, c, 1).wait_send())

    @pl.when(second)
    def _():
        each(1, OWNERS, lambda k: gather(k).wait_send())

        @pl.when(y >= 2)
        def _():
            gather(0).wait_send()


def hbm(x):
    return pltpu.with_memory_space_constraint(x, pltpu.HBM)


def fold(x):
    cells = x.shape[2]
    x = x.reshape(2, NV, cells // (4 * LANES), 4, LANES).transpose(1, 2, 3, 0, 4)
    return x.reshape(NV, cells // (4 * LANES), 8, LANES)


def unfold(x):
    x = x.reshape(NV, x.shape[1], 4, 2, LANES).transpose(3, 0, 1, 2, 4)
    return x.reshape(2, NV, -1)


def fold_jacobian(x):
    cells = x.shape[3]
    x = x.reshape(2, NV, NV, cells // (8 * LANES), 8, LANES).transpose(1, 2, 3, 4, 0, 5)
    return x.reshape(NV, NV, cells // (8 * LANES), 16, LANES)


def shards(adjoint, jacobian, source_term, face_area, face_band, partition_row):
    cells, faces = adjoint.shape[2], face_area.shape[0]
    groups = cells // (4 * LANES)
    assert groups == GROUP * CHUNKS
    f32, bf16, i32 = jnp.float32, jnp.bfloat16, jnp.int32
    dma = pltpu.SemaphoreType.DMA
    state = pltpu.VMEM((NV, groups, 8, LANES), f32)
    box = pltpu.VMEM((16, LANES), f32)
    boxes = pltpu.VMEM((OWNERS, 16, LANES), f32)
    updated = pl.pallas_call(
        kernel,
        out_shape=pltpu.VMEM((NV, groups, 8, LANES), f32),
        in_specs=[pl.BlockSpec(memory_space=pl.ANY)] * 5 + [pl.BlockSpec(memory_space=pltpu.SMEM)],
        out_specs=pl.BlockSpec(memory_space=pltpu.VMEM),
        scratch_shapes=[
            state,
            pltpu.VMEM((NV, NV, groups // 2, 16, LANES), bf16),
            state,
            state,
            pltpu.VMEM((2, NV, groups, 8, LANES), f32),
            state,
            pltpu.VMEM((NV, RAW * GROUP, 8, LANES), f32),
            pltpu.VMEM((faces // LANES, LANES), f32),
            pltpu.VMEM((faces // LANES, LANES), i32),
            pltpu.VMEM((BANDS, faces), bf16),
            pltpu.VMEM((32, faces), f32),
            boxes,
            boxes,
            box,
            box,
            box,
            pltpu.VMEM((OWNERS // 2, 16, LANES), f32),
            pltpu.SemaphoreType.REGULAR,
            dma((6,)),
            dma((CHUNKS,)),
            dma((CHUNKS,)),
            dma((2, CHUNKS)),
            dma((CHUNKS,)),
            dma((RAW,)),
            dma((RAW,)),
            dma((OWNERS,)),
            dma((OWNERS,)),
            dma,
            dma,
            dma((OWNERS,)),
            dma((OWNERS // 2,)),
        ],
        compiler_params=pltpu.CompilerParams(
            collective_id=0, has_side_effects=True, vmem_limit_bytes=40 << 20
        ),
    )(
        hbm(fold(adjoint)),
        hbm(fold_jacobian(jacobian)),
        hbm(fold(source_term)),
        hbm(face_area.reshape(faces // LANES, LANES)),
        hbm(face_band.reshape(faces // LANES, LANES)),
        partition_row,
    )
    return unfold(updated)


def solution(mesh):
    placed = (
        P("inst", None, "rows"),
        P("inst", None, None, "rows"),
        P("inst", None, "rows"),
        P("rows"),
        P("rows"),
        P("rows"),
    )
    return jax.shard_map(
        shards, mesh=mesh, in_specs=placed, out_specs=P("inst", None, "rows"), check_vma=False
    )
```

time: 36.2 us -> 24.2 us (0.67)
  Pallas kernels: 33.3 us -> 22.6 us
  local copies, waits for them, and re-layouts: 2.03 us -> 0.87 us
    pallas_call x1, Pallas kernels: 33.3 us -> 22.6 us  [shards(): pl.pallas_call(kernel, out_shape=pltpu.VMEM((NV, groups, 8, LANES), f32),...]
    unnamed x1, local copies, waits for them, and re-layouts: 2.03 us -> 0.87 us
where the time goes in v2:
time: 24.2 us; the launch traced here: 24.1 us
  Pallas kernels  22.6 us (93%)
  local copies, waits for them, and re-layouts  0.87 us (4%)
  between operations  0.66 us (3%)
    pallas_call x1, Pallas kernels, shards(): pl.pallas_call(kernel, out_shape=pltpu.VMEM((NV, groups, 8, LANES), f32),...  22.6 us
    unnamed x1, local copies, waits for them, and re-layouts  0.87 us

profile of v2, /device:TPU:0, one launch (start us, length us, event | category | flops | bytes accessed | tf_op | source)
XLA Modules:
  0.0 24.1 jit_solution(15882841102249866301)
XLA Ops:
  0.7 22.6 %shard_map.64 = f32[5,36,8,128]{3,2,1,0:T(8,128)S(1)} custom-call(f32[5,36,8,128]{3,2,1,0:T(8,128)} %bitcast.24, bf16[5,5,18,16,128]{4,3,2,1,0:T(8,128)(2,1)} %bitcast.23, f32[5,36,8,128]{3,2,1,0:T(8,128)} %bitcast.25, f32[32,128]{1,0:T(8,128)} %bitcast.26, s32[32,128]{1,0:T(8,128)} %bitcast.27, s32[1]{0:T(128)S(6)} %copy.13.owner), custom_call_target="tpu_custom_call" | custom-call | tf_op jit(solution)/shard_map/pallas_call | solution.py:392
  23.3 0.9 %copy.12 = f32[2,5,18432]{2,0,1:T(2,128)} copy(f32[2,5,18432]{2,0,1:T(2,128)S(1)} %bitcast.22) | data formatting | bytes 1474560

commit v3 on v2

--- a/solution.py
+++ b/solution.py
@@ -24,6 +24,13 @@
 OWNERS = 16
 
 
+def ring(k):
+    return min(k, 4 - k)
+
+
+FAR_FIRST = sorted(range(1, OWNERS), key=lambda k: -ring(k // 4) - ring(k % 4))
+
+
 def spectral(offset):
     if offset % NT == 0:
         return 0.0
@@ -53,7 +60,7 @@
 def kernel(
     adjoint, jacobian, source, area, band, owner, result,
     own, jac, src, sibling, outbox, inbox, relay, area_v, band_v,
-    table, weighted, part, gathered, half_sum, other_sum, total, means,
+    table, index, weighted, part, gathered, half_sum, other_sum, total, means,
     near_sem, local_sem, sib_send, sib_recv, link_send, link_recv, relay_send, relay_recv,
     rs_send, rs_recv, x_send, x_recv, ag_send, ag_recv,
 ):
@@ -63,7 +70,6 @@
     first, second = core == 0, core == 1
     sibling_id = (rows, inst + 1 - 2 * core)
     link_id = (rows, (inst + 2) % 4)
-    diagonal_id = (rows, (inst + 2) % 4 + 1 - 2 * core)
     across_id = (z * 8 + (1 - x_hi) * 4 + y, inst)
     me = z * 4 + y
     faces = weighted.shape[1]
@@ -143,7 +149,9 @@
     @pl.when(second)
     def _():
         signal(barrier, sibling_id)
-        signal(barrier, diagonal_id)
+        for k in FAR_FIRST:
+            signal(barrier, device(k, inst))
+        signal(barrier, across_id)
 
     tail, front = pl.ds(face_start, face_groups), pl.ds(0, face_start)
     got_faces = fetch(0, adjoint.at[:, tail], own.at[:, tail])
@@ -155,8 +163,9 @@
 
     @pl.when(first)
     def _():
-        pl.semaphore_wait(barrier, 3)
+        pl.semaphore_wait(barrier, 2)
         signal(near_sem, sibling_id)
+        signal(near_sem, link_id)
         each(0, RAW, lambda c: to_link(adjoint, c, 0).start())
         each(face_chunk, CHUNKS, lambda c: to_sibling(c).start())
         each(0, face_chunk, lambda c: to_sibling(c).start())
@@ -164,13 +173,18 @@
     @pl.when(second)
     def _():
         pl.semaphore_wait(near_sem, 1)
-        each(1, OWNERS, lambda k: signal(barrier, device(k, inst)))
-        signal(barrier, across_id)
         each(0, CHUNKS, lambda c: to_sibling(c).start())
 
     got_area.wait()
     got_band.wait()
     band_index = lax.broadcasted_iota(jnp.int32, (BANDS, LANES), 0)
+    block_row = lax.broadcasted_iota(jnp.int32, (8, LANES), 0)
+
+    def locate(g):
+        bands = band_v[pl.ds(4 * g, 1), :]
+        for r in range(1, 4):
+            bands = jnp.where(block_row < 2 * r, bands, band_v[pl.ds(4 * g + r, 1), :])
+        index[g] = bands
 
     def mark(n):
         here = pl.ds(pl.multiple_of(n * LANES, LANES), LANES)
@@ -220,9 +234,10 @@
                     16 * (q // 2) : 16 * (q // 2) + 16, LANES * (q % 2) : LANES * (q % 2 + 1)
                 ]
         pl.semaphore_wait(barrier, OWNERS)
-        each(1, OWNERS, lambda k: scatter(k).start())
-
-    odd = lax.broadcasted_iota(jnp.int32, (8, LANES), 0) % 2 == 1
+        for k in FAR_FIRST:
+            scatter(k).start()
+
+    odd = block_row % 2 == 1
 
     def weights(by_offset):
         return by_offset[0], jnp.where(odd, by_offset[1], by_offset[-1])
@@ -253,12 +268,12 @@
                 a, b = own[v, span(c)], sibling[v, span(c)]
                 outbox[0, v, span(c)] = combine(a, b, facing, down)
                 outbox[1, v, span(c)] = combine(b, a, facing, up)
+            to_link(outbox.at[1], c, 1).start()
             to_link(outbox.at[0], c, 0).start()
-            to_link(outbox.at[1], c, 1).start()
-
+
+        pl.semaphore_wait(near_sem, 1)
         each(0, RAW, send_raw)
         each(RAW, CHUNKS, send_partial)
-        each(0, faces // LANES, mark)
 
     @pl.when(second)
     def _():
@@ -281,18 +296,20 @@
             result[v, here] = state[v] + coupled - pseudo_step * (flux - src[v, here])
 
     each(0, CHUNKS, base)
-
-    @pl.when(second)
-    def _():
-        each(1, OWNERS, lambda k: scatter(k).wait())
+    each(0, face_groups, locate)
+
+    @pl.when(second)
+    def _():
+        each(1, OWNERS, lambda k: scatter(k).wait_recv())
         sum_here = part[me]
         for k in range(1, OWNERS):
             sum_here = sum_here + gathered[k]
         half_sum[...] = sum_here
         across.start()
-        across.wait()
+        across.wait_recv()
         total[...] = half_sum[...] + other_sum[...]
-        each(1, OWNERS, lambda k: gather(k).start())
+        for k in FAR_FIRST:
+            gather(k).start()
 
         @pl.when(y >= 2)
         def _():
@@ -321,26 +338,34 @@
 
     each(RAW, face_chunk, finish)
 
+    odd_wide = lax.broadcasted_iota(jnp.int32, (8, BANDS), 0) % 2 == 1
     each(0, OWNERS // 2, lambda n: arrived(n).wait_recv())
     for h in range(2):
-        table_sum = 0.0
+        sums = 0.0
         for p in range(PLANES):
-            table_sum += jnp.concatenate([means[2 * p], means[2 * p + 1]], axis=1) * on_plane[h][p]
-        total_area = table_sum[2 * NV : 2 * NV + 1]
-        total_area = jnp.where(total_area > 0, total_area, 1.0)
-        cut = slice(h * half, (h + 1) * half)
-        both = jnp.dot(split(table_sum / total_area), table[:, cut], preferred_element_type=jnp.float32)
-        weighted[0:16, cut] = (both[0:16] + both[16:32]) * (pseudo_step * coupling_gain)
-
-    def mix(g):
-        here = face_start + g
-        for v in range(NV):
-            result[v, here] += own[v, here] * (pseudo_step * coupling_gain)
-            for r in range(4):
-                lanes = pl.ds(pl.multiple_of((4 * g + r) * LANES, LANES), LANES)
-                result[v, here, 2 * r : 2 * r + 2, :] -= weighted[2 * v : 2 * v + 2, lanes]
-
-    each(0, face_groups, mix)
+            sums += jnp.concatenate([means[2 * p], means[2 * p + 1]], axis=1) * on_plane[h][p]
+        total_area = sums[2 * NV : 2 * NV + 1]
+        mean = sums / jnp.where(total_area > 0, total_area, 1.0)
+        mean = mean * (pseudo_step * coupling_gain)
+        by_row = [
+            jnp.where(odd_wide, mean[2 * v + 1 : 2 * v + 2], mean[2 * v : 2 * v + 1]) for v in range(NV)
+        ]
+
+        def mix(n):
+            g = h * (face_groups // 2) + n
+            here = face_start + g
+            band = index[g]
+            lane = band % LANES
+            for v in range(NV):
+                face_mean = jnp.where(
+                    band < LANES,
+                    jnp.take_along_axis(by_row[v][:, :LANES], lane, axis=1, mode="promise_in_bounds"),
+                    jnp.take_along_axis(by_row[v][:, LANES:], lane, axis=1, mode="promise_in_bounds"),
+                )
+                result[v, here] += own[v, here] * (pseudo_step * coupling_gain) - face_mean
+
+        each(0, face_groups // 2, mix)
+
     each(face_chunk, CHUNKS, finish)
 
     each(0, CHUNKS, lambda c: to_sibling(c).wait_send())
@@ -352,6 +377,8 @@
 
     @pl.when(second)
     def _():
+        each(1, OWNERS, lambda k: scatter(k).wait_send())
+        across.wait_send()
         each(1, OWNERS, lambda k: gather(k).wait_send())
 
         @pl.when(y >= 2)
@@ -405,6 +432,7 @@
             pltpu.VMEM((faces // LANES, LANES), f32),
             pltpu.VMEM((faces // LANES, LANES), i32),
             pltpu.VMEM((BANDS, faces), bf16),
+            pltpu.VMEM((faces // (4 * LANES), 8, LANES), i32),
             pltpu.VMEM((32, faces), f32),
             boxes,
             boxes,

time: 24.2 us -> 22.9 us (0.946); the launches traced: 24.1 us -> 22.5 us
  Pallas kernels: 22.6 us -> 21 us
    pallas_call x1, Pallas kernels: 22.6 us -> 21 us  [shards(): pl.pallas_call(kernel, out_shape=pltpu.VMEM((NV, groups, 8, LANES), f32),...]
where the time goes in v3:
time: 22.9 us; the launch traced here: 22.5 us
  Pallas kernels  21 us (92%)
  local copies, waits for them, and re-layouts  0.87 us (4%)
  between operations  0.66 us (3%)
    pallas_call x1, Pallas kernels, shards(): pl.pallas_call(kernel, out_shape=pltpu.VMEM((NV, groups, 8, LANES), f32),...  21 us
    unnamed x1, local copies, waits for them, and re-layouts  0.87 us

profile of v3, /device:TPU:0, one launch (start us, length us, event | category | flops | bytes accessed | tf_op | source)
XLA Modules:
  0.0 22.5 jit_solution(14877661734314441816)
XLA Ops:
  0.7 21.0 %shard_map.64 = f32[5,36,8,128]{3,2,1,0:T(8,128)S(1)} custom-call(f32[5,36,8,128]{3,2,1,0:T(8,128)} %bitcast.24, bf16[5,5,18,16,128]{4,3,2,1,0:T(8,128)(2,1)} %bitcast.23, f32[5,36,8,128]{3,2,1,0:T(8,128)} %bitcast.25, f32[32,128]{1,0:T(8,128)} %bitcast.26, s32[32,128]{1,0:T(8,128)} %bitcast.27, s32[1]{0:T(128)S(6)} %copy.13.owner), custom_call_target="tpu_custom_call" | custom-call | tf_op jit(solution)/shard_map/pallas_call | solution.py:419
  21.6 0.9 %copy.12 = f32[2,5,18432]{2,0,1:T(2,128)} copy(f32[2,5,18432]{2,0,1:T(2,128)S(1)} %bitcast.22) | data formatting | bytes 1474560

commit v4 on v3

--- a/solution.py
+++ b/solution.py
@@ -18,9 +18,11 @@
 coupling_gain = 2.0
 pseudo_step = 0.5
 
-GROUP = 4
-CHUNKS = 9
-RAW = 2
+SENDER = 0
+GROUPS = 36
+RAW = 8
+PARTS = 4
+PART = (GROUPS - RAW) // PARTS
 OWNERS = 16
 
 
@@ -59,15 +61,15 @@
 
 def kernel(
     adjoint, jacobian, source, area, band, owner, result,
-    own, jac, src, sibling, outbox, inbox, relay, area_v, band_v,
+    own, jac, src, sibling, outbox, inbox, raw, relay, area_v, band_v,
     table, index, weighted, part, gathered, half_sum, other_sum, total, means,
-    near_sem, local_sem, sib_send, sib_recv, link_send, link_recv, relay_send, relay_recv,
+    near_sem, local_sem, sib_send, sib_recv, raw_send, raw_recv, link_send, link_recv, relay_send, relay_recv,
     rs_send, rs_recv, x_send, x_recv, ag_send, ag_recv,
 ):
     rows, inst = lax.axis_index("rows"), lax.axis_index("inst")
     z, x_hi, y = rows // 8, (rows // 4) % 2, rows % 4
     core = inst % 2
-    first, second = core == 0, core == 1
+    sender, agent = core == SENDER, core != SENDER
     sibling_id = (rows, inst + 1 - 2 * core)
     link_id = (rows, (inst + 2) % 4)
     across_id = (z * 8 + (1 - x_hi) * 4 + y, inst)
@@ -75,8 +77,8 @@
     faces = weighted.shape[1]
     half = faces // 2
     face_groups = faces // (4 * LANES)
-    face_start = GROUP * CHUNKS - face_groups
-    face_chunk = face_start // GROUP
+    face_start = GROUPS - face_groups
+    cuts = ((face_start, GROUPS), (0, face_start)), ((0, RAW), (RAW, RAW + PART), (RAW + PART, GROUPS))
 
     def place(k):
         return (z + k // 4) % 4, (y + k % 4) % 4
@@ -85,8 +87,8 @@
         zd, yd = place(k)
         return (zd * 8 + x_hi * 4 + yd, inst)
 
-    def span(c):
-        return pl.ds(c * GROUP, GROUP)
+    def span(n):
+        return pl.ds(RAW + n * PART, PART)
 
     def each(low, high, act):
         def body(k, carry):
@@ -100,6 +102,9 @@
         copy.start()
         return copy
 
+    def drain(like, sem):
+        pltpu.make_async_copy(like, like, sem).wait()
+
     def signal(sem, device_id):
         pl.semaphore_signal(sem, inc=1, device_id=device_id, device_id_type=MESH)
 
@@ -108,45 +113,51 @@
             a, b, send, recv, device_id=device_id, device_id_type=MESH
         )
 
-    def to_sibling(c):
-        return remote(
-            adjoint.at[:, span(c)], sibling.at[:, span(c)], sib_send.at[c], sib_recv.at[c], sibling_id
-        )
-
-    def to_link(source_ref, c, core_there):
-        target = (rows, (inst + 2) % 4 + core_there)
-        return remote(
-            source_ref.at[:, span(c)], inbox.at[:, span(c)], link_send.at[core_there, c], link_recv.at[c], target
-        )
-
-    def to_relay(c):
-        return remote(inbox.at[:, span(c)], relay.at[:, span(c)], relay_send.at[c], relay_recv.at[c], sibling_id)
+    def give(pieces):
+        for n, (low, high) in enumerate(pieces):
+            here = pl.ds(low, high - low)
+            remote(adjoint.at[:, here], sibling.at[:, here], sib_send, sib_recv.at[n], sibling_id).start()
+
+    def given(pieces, n):
+        low, high = pieces[n]
+        drain(sibling.at[:, pl.ds(low, high - low)], sib_recv.at[n])
+
+    def beyond(other):
+        return (rows, (inst + 2) % 4 + other * (1 - 2 * core))
+
+    def raw_to_link(given, other):
+        here = given.at[:, pl.ds(0, RAW)]
+        return remote(here, raw, raw_send.at[other], raw_recv, beyond(other))
+
+    def to_link(n, other):
+        arrival = link_recv.at[n // (PARTS - 1)]
+        return remote(outbox.at[other, n], inbox.at[n], link_send, arrival, beyond(other))
+
+    def to_relay():
+        return remote(raw, relay, relay_send, relay_recv, sibling_id)
 
     def scatter(k):
         zd, yd = place(k)
-        return remote(part.at[zd * 4 + yd], gathered.at[k], rs_send.at[k], rs_recv.at[k], device(k, inst))
+        return remote(part.at[zd * 4 + yd], gathered.at[k], rs_send, rs_recv, device(k, inst))
 
     slot = 2 * z + y % 2
-    served = inst - y // 2
+    served = inst + (y // 2) * (1 - 2 * core)
 
     def gather(k):
-        return remote(total, means.at[slot], ag_send.at[k], ag_recv.at[slot], device(k, served))
+        return remote(total, means.at[slot], ag_send, ag_recv, device(k, served))
 
     def keep():
-        return pltpu.make_async_copy(total, means.at[slot], ag_recv.at[slot])
-
-    def arrived(n):
-        return remote(total, means.at[n], ag_send.at[0], ag_recv.at[n], sibling_id)
+        return pltpu.make_async_copy(total, means.at[slot], ag_recv)
 
     across = remote(half_sum, other_sum, x_send, x_recv, across_id)
 
     barrier = pltpu.get_barrier_semaphore()
 
-    @pl.when(first)
+    @pl.when(sender)
     def _():
         signal(barrier, link_id)
 
-    @pl.when(second)
+    @pl.when(agent)
     def _():
         signal(barrier, sibling_id)
         for k in FAR_FIRST:
@@ -161,19 +172,18 @@
     got_jac = fetch(4, jacobian, jac)
     got_src = fetch(5, source, src)
 
-    @pl.when(first)
+    @pl.when(sender)
     def _():
         pl.semaphore_wait(barrier, 2)
         signal(near_sem, sibling_id)
         signal(near_sem, link_id)
-        each(0, RAW, lambda c: to_link(adjoint, c, 0).start())
-        each(face_chunk, CHUNKS, lambda c: to_sibling(c).start())
-        each(0, face_chunk, lambda c: to_sibling(c).start())
-
-    @pl.when(second)
+        raw_to_link(adjoint, 0).start()
+        give(cuts[0])
+
+    @pl.when(agent)
     def _():
         pl.semaphore_wait(near_sem, 1)
-        each(0, CHUNKS, lambda c: to_sibling(c).start())
+        give(cuts[1])
 
     got_area.wait()
     got_band.wait()
@@ -211,13 +221,13 @@
 
         each(0, face_groups, group)
 
-    @pl.when(second)
+    @pl.when(agent)
     def _():
         each(0, faces // LANES, mark)
         weighted[...] = jnp.zeros_like(weighted)
         got_faces.wait()
         weigh(own, 0)
-        each(face_chunk, CHUNKS, lambda c: to_sibling(c).wait_recv())
+        given(cuts[0], 0)
         weigh(sibling, 16)
         sums = []
         for h in range(2):
@@ -245,62 +255,60 @@
     shifts = (-1, 0, 1)
     inner = weights({d: weight_of(d) for d in shifts})
     facing = weights({d: weight_of(4 + d) for d in shifts})
-    up = weights({d: weight_of(2 + d) for d in shifts})
-    down = weights({d: weight_of(-2 + d) for d in shifts})
-    near = weights({d: pick(first, weight_of(2 + d), weight_of(-2 + d)) for d in shifts})
-    away = weights({d: pick(first, weight_of(-2 + d), weight_of(2 + d)) for d in shifts})
+    skew = 2 if SENDER else -2
+    for_facing = weights({d: weight_of(skew + d) for d in shifts})
+    for_other = weights({d: weight_of(-skew + d) for d in shifts})
+    near = weights({d: pick(core == 0, weight_of(2 + d), weight_of(-2 + d)) for d in shifts})
+    away = weights({d: pick(core == 0, weight_of(-2 + d), weight_of(2 + d)) for d in shifts})
 
     def combine(a, b, wa, wb):
         return wa[0] * a + wb[0] * b + swap(wa[1] * a + wb[1] * b)
 
-    @pl.when(first)
-    def _():
+    @pl.when(sender)
+    def _():
+        pl.semaphore_wait(near_sem, 1)
+        given(cuts[1], 0)
+        raw_to_link(sibling, 1).start()
         got_front.wait()
         got_faces.wait()
-
-        def send_raw(c):
-            to_sibling(c).wait_recv()
-            to_link(sibling, c, 1).start()
-
-        def send_partial(c):
-            to_sibling(c).wait_recv()
-            for v in range(NV):
-                a, b = own[v, span(c)], sibling[v, span(c)]
-                outbox[0, v, span(c)] = combine(a, b, facing, down)
-                outbox[1, v, span(c)] = combine(b, a, facing, up)
-            to_link(outbox.at[1], c, 1).start()
-            to_link(outbox.at[0], c, 0).start()
-
-        pl.semaphore_wait(near_sem, 1)
-        each(0, RAW, send_raw)
-        each(RAW, CHUNKS, send_partial)
-
-    @pl.when(second)
-    def _():
-        each(0, face_chunk, lambda c: to_sibling(c).wait_recv())
+        for n in range(PARTS):
+            if n < 2:
+                given(cuts[1], n + 1)
+
+            def mix_instances(v):
+                a, b = own[v, span(n)], sibling[v, span(n)]
+                outbox[1, n, v] = combine(b, a, facing, for_other)
+                outbox[0, n, v] = combine(a, b, facing, for_facing)
+
+            each(0, NV, mix_instances)
+            to_link(n, 1).start()
+            to_link(n, 0).start()
+
+    @pl.when(agent)
+    def _():
+        given(cuts[0], 1)
         got_front.wait()
 
     got_jac.wait()
     got_src.wait()
 
-    def base(c):
-        here = span(c)
-        half_groups = pl.ds(c * (GROUP // 2), GROUP // 2)
+    def base(m):
+        here = pl.ds(4 * m, 4)
         state = [own[w, here] for w in range(NV)]
         for v in range(NV):
             flux = 0.0
             for w in range(NV):
-                block = jac[w, v, half_groups].astype(jnp.float32).reshape(GROUP, 8, LANES)
+                block = jac[w, v, pl.ds(2 * m, 2)].astype(jnp.float32).reshape(4, 8, LANES)
                 flux = flux + block * state[w]
             coupled = combine(state[v], sibling[v, here], inner, near)
             result[v, here] = state[v] + coupled - pseudo_step * (flux - src[v, here])
 
-    each(0, CHUNKS, base)
+    each(0, GROUPS // 4, base)
     each(0, face_groups, locate)
 
-    @pl.when(second)
-    def _():
-        each(1, OWNERS, lambda k: scatter(k).wait_recv())
+    @pl.when(agent)
+    def _():
+        drain(gathered.at[pl.ds(1, OWNERS - 1)], rs_recv)
         sum_here = part[me]
         for k in range(1, OWNERS):
             sum_here = sum_here + gathered[k]
@@ -319,27 +327,21 @@
         def _():
             keep().start()
 
-    def pass_on(c):
-        to_link(inbox, c, 0).wait_recv()
-        to_relay(c).start()
-
-    each(0, RAW, pass_on)
-
-    def finish_raw(c):
-        to_relay(c).wait()
-        for v in range(NV):
-            result[v, span(c)] += combine(inbox[v, span(c)], relay[v, span(c)], facing, away)
-
-    each(0, RAW, finish_raw)
-
-    def finish(c):
-        to_link(inbox, c, 0).wait_recv()
-        result[:, span(c)] += inbox[:, span(c)]
-
-    each(RAW, face_chunk, finish)
+    raw_to_link(adjoint, 0).wait_recv()
+    to_relay().start()
+
+    def finish(n):
+        result[:, span(n)] += inbox[n]
+
+    drain(inbox.at[pl.ds(0, PARTS - 1)], link_recv.at[0])
+    each(0, PARTS - 1, finish)
+
+    to_relay().wait()
+    for v in range(NV):
+        result[v, 0:RAW] += combine(raw[v], relay[v], facing, away)
 
     odd_wide = lax.broadcasted_iota(jnp.int32, (8, BANDS), 0) % 2 == 1
-    each(0, OWNERS // 2, lambda n: arrived(n).wait_recv())
+    drain(means, ag_recv)
     for h in range(2):
         sums = 0.0
         for p in range(PLANES):
@@ -366,24 +368,29 @@
 
         each(0, face_groups // 2, mix)
 
-    each(face_chunk, CHUNKS, finish)
-
-    each(0, CHUNKS, lambda c: to_sibling(c).wait_send())
-
-    @pl.when(first)
-    def _():
-        each(0, CHUNKS, lambda c: to_link(inbox, c, 0).wait_send())
-        each(0, CHUNKS, lambda c: to_link(inbox, c, 1).wait_send())
-
-    @pl.when(second)
-    def _():
-        each(1, OWNERS, lambda k: scatter(k).wait_send())
+    drain(inbox.at[PARTS - 1], link_recv.at[1])
+    finish(PARTS - 1)
+
+    drain(sibling, sib_send)
+
+    @pl.when(sender)
+    def _():
+        for other in range(2):
+            raw_to_link(adjoint, other).wait_send()
+        drain(outbox, link_send)
+
+    @pl.when(agent)
+    def _():
         across.wait_send()
-        each(1, OWNERS, lambda k: gather(k).wait_send())
+        drain(gathered.at[pl.ds(1, OWNERS - 1)], rs_send)
 
         @pl.when(y >= 2)
         def _():
-            gather(0).wait_send()
+            drain(gathered, ag_send)
+
+        @pl.when(y < 2)
+        def _():
+            drain(gathered.at[pl.ds(1, OWNERS - 1)], ag_send)
 
 
 def hbm(x):
@@ -410,7 +417,7 @@
 def shards(adjoint, jacobian, source_term, face_area, face_band, partition_row):
     cells, faces = adjoint.shape[2], face_area.shape[0]
     groups = cells // (4 * LANES)
-    assert groups == GROUP * CHUNKS
+    assert groups == GROUPS
     f32, bf16, i32 = jnp.float32, jnp.bfloat16, jnp.int32
     dma = pltpu.SemaphoreType.DMA
     state = pltpu.VMEM((NV, groups, 8, LANES), f32)
@@ -426,9 +433,10 @@
             pltpu.VMEM((NV, NV, groups // 2, 16, LANES), bf16),
             state,
             state,
-            pltpu.VMEM((2, NV, groups, 8, LANES), f32),
-            state,
-            pltpu.VMEM((NV, RAW * GROUP, 8, LANES), f32),
+            pltpu.VMEM((2, PARTS, NV, PART, 8, LANES), f32),
+            pltpu.VMEM((PARTS, NV, PART, 8, LANES), f32),
+            pltpu.VMEM((NV, RAW, 8, LANES), f32),
+            pltpu.VMEM((NV, RAW, 8, LANES), f32),
             pltpu.VMEM((faces // LANES, LANES), f32),
             pltpu.VMEM((faces // LANES, LANES), i32),
             pltpu.VMEM((BANDS, faces), bf16),
@@ -442,18 +450,20 @@
             pltpu.VMEM((OWNERS // 2, 16, LANES), f32),
             pltpu.SemaphoreType.REGULAR,
             dma((6,)),
-            dma((CHUNKS,)),
-            dma((CHUNKS,)),
-            dma((2, CHUNKS)),
-            dma((CHUNKS,)),
-            dma((RAW,)),
-            dma((RAW,)),
-            dma((OWNERS,)),
-            dma((OWNERS,)),
-            dma,
-            dma,
-            dma((OWNERS,)),
-            dma((OWNERS // 2,)),
+            dma,
+            dma((3,)),
+            dma((2,)),
+            dma,
+            dma,
+            dma((2,)),
+            dma,
+            dma,
+            dma,
+            dma,
+            dma,
+            dma,
+            dma,
+            dma,
         ],
         compiler_params=pltpu.CompilerParams(
             collective_id=0, has_side_effects=True, vmem_limit_bytes=40 << 20

time: 22.9 us -> 21.9 us (0.956)
  Pallas kernels: 21 us -> 20 us
    pallas_call x1, Pallas kernels: 21 us -> 20 us  [shards(): pl.pallas_call(kernel, out_shape=pltpu.VMEM((NV, groups, 8, LANES), f32),...]
where the time goes in v4:
time: 21.9 us; the launch traced here: 21.5 us
  Pallas kernels  20 us (91%)
  local copies, waits for them, and re-layouts  0.87 us (4%)
  between operations  0.66 us (3%)
    pallas_call x1, Pallas kernels, shards(): pl.pallas_call(kernel, out_shape=pltpu.VMEM((NV, groups, 8, LANES), f32),...  20 us
    unnamed x1, local copies, waits for them, and re-layouts  0.87 us

profile of v4, /device:TPU:0, one launch (start us, length us, event | category | flops | bytes accessed | tf_op | source)
XLA Modules:
  0.0 21.5 jit_solution(10483295251788972671)
XLA Ops:
  0.7 20.0 %shard_map.64 = f32[5,36,8,128]{3,2,1,0:T(8,128)S(1)} custom-call(f32[5,36,8,128]{3,2,1,0:T(8,128)} %bitcast.24, bf16[5,5,18,16,128]{4,3,2,1,0:T(8,128)(2,1)} %bitcast.23, f32[5,36,8,128]{3,2,1,0:T(8,128)} %bitcast.25, f32[32,128]{1,0:T(8,128)} %bitcast.26, s32[32,128]{1,0:T(8,128)} %bitcast.27, s32[1]{0:T(128)S(6)} %copy.13.owner), custom_call_target="tpu_custom_call" | custom-call | tf_op jit(solution)/shard_map/pallas_call | solution.py:426
  20.7 0.9 %copy.12 = f32[2,5,18432]{2,0,1:T(2,128)} copy(f32[2,5,18432]{2,0,1:T(2,128)S(1)} %bitcast.22) | data formatting | bytes 1474560

commit v5 on v4

--- a/solution.py
+++ b/solution.py
@@ -78,7 +78,11 @@
     half = faces // 2
     face_groups = faces // (4 * LANES)
     face_start = GROUPS - face_groups
-    cuts = ((face_start, GROUPS), (0, face_start)), ((0, RAW), (RAW, RAW + PART), (RAW + PART, GROUPS))
+    face_middle = face_start + face_groups // 2
+    cuts = (
+        ((face_start, face_middle), (face_middle, GROUPS), (0, face_start)),
+        ((0, RAW), (RAW, RAW + PART), (RAW + PART, GROUPS)),
+    )
 
     def place(k):
         return (z + k // 4) % 4, (y + k % 4) % 4
@@ -98,9 +102,7 @@
         lax.fori_loop(low, high, body, 0)
 
     def fetch(k, a, b):
-        copy = pltpu.make_async_copy(a, b, local_sem.at[k])
-        copy.start()
-        return copy
+        return pltpu.make_async_copy(a, b, local_sem.at[k])
 
     def drain(like, sem):
         pltpu.make_async_copy(like, like, sem).wait()
@@ -125,13 +127,13 @@
     def beyond(other):
         return (rows, (inst + 2) % 4 + other * (1 - 2 * core))
 
-    def raw_to_link(given, other):
-        here = given.at[:, pl.ds(0, RAW)]
+    def raw_to_link(state, other):
+        here = state.at[:, pl.ds(0, RAW)]
         return remote(here, raw, raw_send.at[other], raw_recv, beyond(other))
 
     def to_link(n, other):
         arrival = link_recv.at[n // (PARTS - 1)]
-        return remote(outbox.at[other, n], inbox.at[n], link_send, arrival, beyond(other))
+        return remote(outbox.at[other * PARTS + n], inbox.at[n], link_send, arrival, beyond(other))
 
     def to_relay():
         return remote(raw, relay, relay_send, relay_recv, sibling_id)
@@ -164,30 +166,41 @@
             signal(barrier, device(k, inst))
         signal(barrier, across_id)
 
-    tail, front = pl.ds(face_start, face_groups), pl.ds(0, face_start)
-    got_faces = fetch(0, adjoint.at[:, tail], own.at[:, tail])
-    got_area = fetch(1, area, area_v)
-    got_band = fetch(2, band, band_v)
-    got_front = fetch(3, adjoint.at[:, front], own.at[:, front])
-    got_jac = fetch(4, jacobian, jac)
-    got_src = fetch(5, source, src)
+    head, middle, tail = pl.ds(0, RAW), pl.ds(RAW, face_start - RAW), pl.ds(face_start, face_groups)
+    got_head = fetch(0, adjoint.at[:, head], own.at[:, head])
+    got_middle = fetch(1, adjoint.at[:, middle], own.at[:, middle])
+    got_faces = fetch(2, adjoint.at[:, tail], own.at[:, tail])
+    got_area = fetch(3, area, area_v)
+    got_band = fetch(4, band, band_v)
+    got_jac = fetch(5, jacobian, jac)
+    got_src = fetch(6, source, src)
 
     @pl.when(sender)
     def _():
+        got_head.start()
+        got_middle.start()
+        got_faces.start()
         pl.semaphore_wait(barrier, 2)
         signal(near_sem, sibling_id)
         signal(near_sem, link_id)
         raw_to_link(adjoint, 0).start()
         give(cuts[0])
+        got_band.start()
+        got_jac.start()
+        got_src.start()
 
     @pl.when(agent)
     def _():
+        got_band.start()
+        got_faces.start()
+        got_area.start()
+        got_head.start()
+        got_middle.start()
+        got_jac.start()
+        got_src.start()
         pl.semaphore_wait(near_sem, 1)
         give(cuts[1])
 
-    got_area.wait()
-    got_band.wait()
-    band_index = lax.broadcasted_iota(jnp.int32, (BANDS, LANES), 0)
     block_row = lax.broadcasted_iota(jnp.int32, (8, LANES), 0)
 
     def locate(g):
@@ -195,10 +208,6 @@
         for r in range(1, 4):
             bands = jnp.where(block_row < 2 * r, bands, band_v[pl.ds(4 * g + r, 1), :])
         index[g] = bands
-
-    def mark(n):
-        here = pl.ds(pl.multiple_of(n * LANES, LANES), LANES)
-        table[:, here] = jnp.where(band_index == band_v[pl.ds(n, 1), :], 1.0, 0.0).astype(jnp.bfloat16)
 
     row = owner[0]
     planes = (jnp.maximum(row - 1, 0), jnp.minimum(row, PLANES - 1))
@@ -207,42 +216,58 @@
         for h in range(2)
     ]
 
-    def weigh(values, top):
+    def turned(x, by):
+        return x if by % 8 == 0 else pltpu.roll(x, by % 8, 0)
+
+    def weigh(values, top, low, high):
         def group(g):
+            blocks = [values[v, face_start + g] for v in range(4)]
             for r in range(4):
-                tile = 4 * g + r
-                here = pl.ds(pl.multiple_of(tile * LANES, LANES), LANES)
-                size = area_v[pl.ds(tile, 1), :]
-                for v in range(NV):
-                    weighted[top + 2 * v : top + 2 * v + 2, here] = (
-                        values[v, face_start + g, 2 * r : 2 * r + 2, :] * size
-                    )
-                weighted[top + 2 * NV : top + 2 * NV + 1, here] = size
-
-        each(0, face_groups, group)
+                here = pl.ds(pl.multiple_of((4 * g + r) * LANES, LANES), LANES)
+                rows = turned(blocks[0], -2 * r)
+                for v in range(1, 4):
+                    rows = jnp.where(block_row // 2 == v, turned(blocks[v], 2 * v - 2 * r), rows)
+                weighted[top : top + 8, here] = rows * area_v[pl.ds(4 * g + r, 1), :]
+
+        each(low, high, group)
+
+    def weigh_last(low, high):
+        def group(g):
+            mine, other = own[NV - 1, face_start + g], sibling[NV - 1, face_start + g]
+            for r in range(4):
+                here = pl.ds(pl.multiple_of((4 * g + r) * LANES, LANES), LANES)
+                rows = jnp.where(block_row < 2, turned(mine, -2 * r), turned(other, 2 - 2 * r))
+                rows = jnp.where(block_row < 4, rows, jnp.where(block_row == 4, 1.0, 0.0))
+                weighted[16:24, here] = rows * area_v[pl.ds(4 * g + r, 1), :]
+
+        each(low, high, group)
 
     @pl.when(agent)
     def _():
-        each(0, faces // LANES, mark)
-        weighted[...] = jnp.zeros_like(weighted)
+        got_band.wait()
+        band_lane = lax.broadcasted_iota(jnp.int32, (LANES, BANDS), 1)
+        by_face = jnp.transpose(band_v[...])
+        for n in range(faces // LANES):
+            here = jnp.where(band_lane == by_face[:, n : n + 1], 1.0, 0.0)
+            table[n * LANES : (n + 1) * LANES, :] = here.astype(jnp.bfloat16)
+        got_area.wait()
         got_faces.wait()
-        weigh(own, 0)
-        given(cuts[0], 0)
-        weigh(sibling, 16)
+        weigh(own, 0, 0, face_groups)
         sums = []
         for h in range(2):
+            given(cuts[0], h)
+            low, high = h * (face_groups // 2), (h + 1) * (face_groups // 2)
+            weigh(sibling, 8, low, high)
+            weigh_last(low, high)
             cut = slice(h * half, (h + 1) * half)
-            both = lax.dot_general(
-                split(weighted[:, cut]), table[:, cut], (((1,), (1,)), ((), ())),
-                preferred_element_type=jnp.float32,
-            )
-            sums.append(both[0:32] + both[32:64])
+            both = jnp.dot(split(weighted[:, cut]), table[cut, :], preferred_element_type=jnp.float32)
+            sums.append(both[0:24] + both[24:48])
         for p in range(PLANES):
             here = sums[0] * on_plane[0][p] + sums[1] * on_plane[1][p]
             for q in range(4):
-                part[4 * p + q] = here[
-                    16 * (q // 2) : 16 * (q // 2) + 16, LANES * (q % 2) : LANES * (q % 2 + 1)
-                ]
+                cut = slice(LANES * (q % 2), LANES * (q % 2 + 1))
+                part[4 * p + q, 0:8] = here[8 * (q // 2) : 8 * (q // 2) + 8, cut]
+                part[4 * p + q, 8:16] = here[16:24, cut]
         pl.semaphore_wait(barrier, OWNERS)
         for k in FAR_FIRST:
             scatter(k).start()
@@ -269,7 +294,8 @@
         pl.semaphore_wait(near_sem, 1)
         given(cuts[1], 0)
         raw_to_link(sibling, 1).start()
-        got_front.wait()
+        got_head.wait()
+        got_middle.wait()
         got_faces.wait()
         for n in range(PARTS):
             if n < 2:
@@ -277,20 +303,13 @@
 
             def mix_instances(v):
                 a, b = own[v, span(n)], sibling[v, span(n)]
-                outbox[1, n, v] = combine(b, a, facing, for_other)
-                outbox[0, n, v] = combine(a, b, facing, for_facing)
+                outbox[PARTS + n, v] = combine(b, a, facing, for_other)
+                outbox[n, v] = combine(a, b, facing, for_facing)
 
             each(0, NV, mix_instances)
             to_link(n, 1).start()
             to_link(n, 0).start()
-
-    @pl.when(agent)
-    def _():
-        given(cuts[0], 1)
-        got_front.wait()
-
-    got_jac.wait()
-    got_src.wait()
+        got_band.wait()
 
     def base(m):
         here = pl.ds(4 * m, 4)
@@ -303,8 +322,15 @@
             coupled = combine(state[v], sibling[v, here], inner, near)
             result[v, here] = state[v] + coupled - pseudo_step * (flux - src[v, here])
 
-    each(0, GROUPS // 4, base)
-    each(0, face_groups, locate)
+    def bases():
+        got_jac.wait()
+        got_src.wait()
+        each(0, GROUPS // 4, base)
+        each(0, face_groups, locate)
+
+    @pl.when(sender)
+    def _():
+        bases()
 
     @pl.when(agent)
     def _():
@@ -314,6 +340,10 @@
             sum_here = sum_here + gathered[k]
         half_sum[...] = sum_here
         across.start()
+        given(cuts[0], 2)
+        got_head.wait()
+        got_middle.wait()
+        bases()
         across.wait_recv()
         total[...] = half_sum[...] + other_sum[...]
         for k in FAR_FIRST:
@@ -346,12 +376,13 @@
         sums = 0.0
         for p in range(PLANES):
             sums += jnp.concatenate([means[2 * p], means[2 * p + 1]], axis=1) * on_plane[h][p]
-        total_area = sums[2 * NV : 2 * NV + 1]
+        total_area = sums[12:13]
         mean = sums / jnp.where(total_area > 0, total_area, 1.0)
         mean = mean * (pseudo_step * coupling_gain)
+        last = jnp.where(agent, mean[8:10], mean[10:12])
         by_row = [
-            jnp.where(odd_wide, mean[2 * v + 1 : 2 * v + 2], mean[2 * v : 2 * v + 1]) for v in range(NV)
-        ]
+            jnp.where(odd_wide, mean[2 * v + 1 : 2 * v + 2], mean[2 * v : 2 * v + 1]) for v in range(4)
+        ] + [jnp.where(odd_wide, last[1:2], last[0:1])]
 
         def mix(n):
             g = h * (face_groups // 2) + n
@@ -433,15 +464,15 @@
             pltpu.VMEM((NV, NV, groups // 2, 16, LANES), bf16),
             state,
             state,
-            pltpu.VMEM((2, PARTS, NV, PART, 8, LANES), f32),
+            pltpu.VMEM((2 * PARTS, NV, PART, 8, LANES), f32),
             pltpu.VMEM((PARTS, NV, PART, 8, LANES), f32),
             pltpu.VMEM((NV, RAW, 8, LANES), f32),
             pltpu.VMEM((NV, RAW, 8, LANES), f32),
             pltpu.VMEM((faces // LANES, LANES), f32),
             pltpu.VMEM((faces // LANES, LANES), i32),
-            pltpu.VMEM((BANDS, faces), bf16),
+            pltpu.VMEM((faces, BANDS), bf16),
             pltpu.VMEM((faces // (4 * LANES), 8, LANES), i32),
-            pltpu.VMEM((32, faces), f32),
+            pltpu.VMEM((24, faces), f32),
             boxes,
             boxes,
             box,
@@ -449,7 +480,7 @@
             box,
             pltpu.VMEM((OWNERS // 2, 16, LANES), f32),
             pltpu.SemaphoreType.REGULAR,
-            dma((6,)),
+            dma((7,)),
             dma,
             dma((3,)),
             dma((2,)),

time: 21.9 us -> 21.8 us (level)
  no operation moved by 1% of the time
where the time goes in v5:
time: 21.8 us; the launch traced here: 21.6 us
  Pallas kernels  20 us (92%)
  local copies, waits for them, and re-layouts  0.87 us (4%)
  between operations  0.66 us (3%)
    pallas_call x1, Pallas kernels, shards(): pl.pallas_call(kernel, out_shape=pltpu.VMEM((NV, groups, 8, LANES), f32),...  20 us
    unnamed x1, local copies, waits for them, and re-layouts  0.87 us

profile of v5, /device:TPU:0, one launch (start us, length us, event | category | flops | bytes accessed | tf_op | source)
XLA Modules:
  0.0 21.6 jit_solution(10097931481899644673)
XLA Ops:
  0.7 20.0 %shard_map.64 = f32[5,36,8,128]{3,2,1,0:T(8,128)S(1)} custom-call(f32[5,36,8,128]{3,2,1,0:T(8,128)} %bitcast.24, bf16[5,5,18,16,128]{4,3,2,1,0:T(8,128)(2,1)} %bitcast.23, f32[5,36,8,128]{3,2,1,0:T(8,128)} %bitcast.25, f32[32,128]{1,0:T(8,128)} %bitcast.26, s32[32,128]{1,0:T(8,128)} %bitcast.27, s32[1]{0:T(128)S(6)} %copy.13.owner), custom_call_target="tpu_custom_call" | custom-call | tf_op jit(solution)/shard_map/pallas_call | solution.py:457
  20.7 0.9 %copy.12 = f32[2,5,18432]{2,0,1:T(2,128)} copy(f32[2,5,18432]{2,0,1:T(2,128)S(1)} %bitcast.22) | data formatting | bytes 1474560

commit v6 on v5

--- a/solution.py
+++ b/solution.py
@@ -63,8 +63,7 @@
     adjoint, jacobian, source, area, band, owner, result,
     own, jac, src, sibling, outbox, inbox, raw, relay, area_v, band_v,
     table, index, weighted, part, gathered, half_sum, other_sum, total, means,
-    near_sem, local_sem, sib_send, sib_recv, raw_send, raw_recv, link_send, link_recv, relay_send, relay_recv,
-    rs_send, rs_recv, x_send, x_recv, ag_send, ag_recv,
+    extent, near_sem, local_sem, sent, sib_recv, raw_recv, link_recv, relay_recv, rs_recv, x_recv, ag_recv,
 ):
     rows, inst = lax.axis_index("rows"), lax.axis_index("inst")
     z, x_hi, y = rows // 8, (rows // 4) % 2, rows % 4
@@ -118,7 +117,7 @@
     def give(pieces):
         for n, (low, high) in enumerate(pieces):
             here = pl.ds(low, high - low)
-            remote(adjoint.at[:, here], sibling.at[:, here], sib_send, sib_recv.at[n], sibling_id).start()
+            remote(adjoint.at[:, here], sibling.at[:, here], sent, sib_recv.at[n], sibling_id).start()
 
     def given(pieces, n):
         low, high = pieces[n]
@@ -129,29 +128,29 @@
 
     def raw_to_link(state, other):
         here = state.at[:, pl.ds(0, RAW)]
-        return remote(here, raw, raw_send.at[other], raw_recv, beyond(other))
+        return remote(here, raw, sent, raw_recv, beyond(other))
 
     def to_link(n, other):
         arrival = link_recv.at[n // (PARTS - 1)]
-        return remote(outbox.at[other * PARTS + n], inbox.at[n], link_send, arrival, beyond(other))
+        return remote(outbox.at[other * PARTS + n], inbox.at[n], sent, arrival, beyond(other))
 
     def to_relay():
-        return remote(raw, relay, relay_send, relay_recv, sibling_id)
+        return remote(raw, relay, sent, relay_recv, sibling_id)
 
     def scatter(k):
         zd, yd = place(k)
-        return remote(part.at[zd * 4 + yd], gathered.at[k], rs_send, rs_recv, device(k, inst))
+        return remote(part.at[zd * 4 + yd], gathered.at[k], sent, rs_recv, device(k, inst))
 
     slot = 2 * z + y % 2
     served = inst + (y // 2) * (1 - 2 * core)
 
     def gather(k):
-        return remote(total, means.at[slot], ag_send, ag_recv, device(k, served))
+        return remote(total, means.at[slot], sent, ag_recv, device(k, served))
 
     def keep():
         return pltpu.make_async_copy(total, means.at[slot], ag_recv)
 
-    across = remote(half_sum, other_sum, x_send, x_recv, across_id)
+    across = remote(half_sum, other_sum, sent, x_recv, across_id)
 
     barrier = pltpu.get_barrier_semaphore()
 
@@ -166,19 +165,17 @@
             signal(barrier, device(k, inst))
         signal(barrier, across_id)
 
-    head, middle, tail = pl.ds(0, RAW), pl.ds(RAW, face_start - RAW), pl.ds(face_start, face_groups)
-    got_head = fetch(0, adjoint.at[:, head], own.at[:, head])
-    got_middle = fetch(1, adjoint.at[:, middle], own.at[:, middle])
-    got_faces = fetch(2, adjoint.at[:, tail], own.at[:, tail])
-    got_area = fetch(3, area, area_v)
-    got_band = fetch(4, band, band_v)
-    got_jac = fetch(5, jacobian, jac)
-    got_src = fetch(6, source, src)
+    front, tail = pl.ds(0, face_start), pl.ds(face_start, face_groups)
+    got_front = fetch(0, adjoint.at[:, front], own.at[:, front])
+    got_faces = fetch(1, adjoint.at[:, tail], own.at[:, tail])
+    got_area = fetch(2, area, area_v)
+    got_band = fetch(3, band, band_v)
+    got_jac = fetch(4, jacobian, jac)
+    got_src = fetch(5, source, src)
 
     @pl.when(sender)
     def _():
-        got_head.start()
-        got_middle.start()
+        got_front.start()
         got_faces.start()
         pl.semaphore_wait(barrier, 2)
         signal(near_sem, sibling_id)
@@ -194,8 +191,7 @@
         got_band.start()
         got_faces.start()
         got_area.start()
-        got_head.start()
-        got_middle.start()
+        got_front.start()
         got_jac.start()
         got_src.start()
         pl.semaphore_wait(near_sem, 1)
@@ -294,8 +290,7 @@
         pl.semaphore_wait(near_sem, 1)
         given(cuts[1], 0)
         raw_to_link(sibling, 1).start()
-        got_head.wait()
-        got_middle.wait()
+        got_front.wait()
         got_faces.wait()
         for n in range(PARTS):
             if n < 2:
@@ -341,8 +336,7 @@
         half_sum[...] = sum_here
         across.start()
         given(cuts[0], 2)
-        got_head.wait()
-        got_middle.wait()
+        got_front.wait()
         bases()
         across.wait_recv()
         total[...] = half_sum[...] + other_sum[...]
@@ -366,7 +360,7 @@
     drain(inbox.at[pl.ds(0, PARTS - 1)], link_recv.at[0])
     each(0, PARTS - 1, finish)
 
-    to_relay().wait()
+    to_relay().wait_recv()
     for v in range(NV):
         result[v, 0:RAW] += combine(raw[v], relay[v], facing, away)
 
@@ -402,26 +396,21 @@
     drain(inbox.at[PARTS - 1], link_recv.at[1])
     finish(PARTS - 1)
 
-    drain(sibling, sib_send)
+    shared = NV * (GROUPS + RAW)
+    by_sender = shared + 2 * NV * GROUPS
+    by_agent = shared + 2 * (2 * OWNERS - 1)
 
     @pl.when(sender)
     def _():
-        for other in range(2):
-            raw_to_link(adjoint, other).wait_send()
-        drain(outbox, link_send)
-
-    @pl.when(agent)
-    def _():
-        across.wait_send()
-        drain(gathered.at[pl.ds(1, OWNERS - 1)], rs_send)
-
-        @pl.when(y >= 2)
-        def _():
-            drain(gathered, ag_send)
-
-        @pl.when(y < 2)
-        def _():
-            drain(gathered.at[pl.ds(1, OWNERS - 1)], ag_send)
+        drain(extent.at[pl.ds(0, by_sender)], sent)
+
+    @pl.when(jnp.logical_and(agent, y < 2))
+    def _():
+        drain(extent.at[pl.ds(0, by_agent)], sent)
+
+    @pl.when(jnp.logical_and(agent, y >= 2))
+    def _():
+        drain(extent.at[pl.ds(0, by_agent + 2)], sent)
 
 
 def hbm(x):
@@ -479,18 +468,13 @@
             box,
             box,
             pltpu.VMEM((OWNERS // 2, 16, LANES), f32),
+            pltpu.VMEM((NV * (3 * GROUPS + RAW), 8, LANES), f32),
             pltpu.SemaphoreType.REGULAR,
-            dma((7,)),
+            dma((6,)),
             dma,
             dma((3,)),
-            dma((2,)),
-            dma,
             dma,
             dma((2,)),
-            dma,
-            dma,
-            dma,
-            dma,
             dma,
             dma,
             dma,

time: 21.8 us -> 21.8 us (level)
  no operation moved by 1% of the time
where the time goes in v6:
time: 21.8 us; the launch traced here: 21.5 us
  Pallas kernels  19.9 us (91%)
  local copies, waits for them, and re-layouts  0.87 us (4%)
  between operations  0.66 us (3%)
    pallas_call x1, Pallas kernels, shards(): pl.pallas_call(kernel, out_shape=pltpu.VMEM((NV, groups, 8, LANES), f32),...  19.9 us
    unnamed x1, local copies, waits for them, and re-layouts  0.87 us

profile of v6, /device:TPU:0, one launch (start us, length us, event | category | flops | bytes accessed | tf_op | source)
XLA Modules:
  0.0 21.5 jit_solution(10350788472557454725)
XLA Ops:
  0.7 19.9 %shard_map.64 = f32[5,36,8,128]{3,2,1,0:T(8,128)S(1)} custom-call(f32[5,36,8,128]{3,2,1,0:T(8,128)} %bitcast.24, bf16[5,5,18,16,128]{4,3,2,1,0:T(8,128)(2,1)} %bitcast.23, f32[5,36,8,128]{3,2,1,0:T(8,128)} %bitcast.25, f32[32,128]{1,0:T(8,128)} %bitcast.26, s32[32,128]{1,0:T(8,128)} %bitcast.27, s32[1]{0:T(128)S(6)} %copy.13.owner), custom_call_target="tpu_custom_call" | custom-call | tf_op jit(solution)/shard_map/pallas_call | solution.py:446
  20.6 0.9 %copy.12 = f32[2,5,18432]{2,0,1:T(2,128)} copy(f32[2,5,18432]{2,0,1:T(2,128)S(1)} %bitcast.22) | data formatting | bytes 1474560

commit v7 on v6

--- a/solution.py
+++ b/solution.py
@@ -178,9 +178,9 @@
         got_front.start()
         got_faces.start()
         pl.semaphore_wait(barrier, 2)
+        raw_to_link(adjoint, 0).start()
         signal(near_sem, sibling_id)
         signal(near_sem, link_id)
-        raw_to_link(adjoint, 0).start()
         give(cuts[0])
         got_band.start()
         got_jac.start()
@@ -243,9 +243,14 @@
         got_band.wait()
         band_lane = lax.broadcasted_iota(jnp.int32, (LANES, BANDS), 1)
         by_face = jnp.transpose(band_v[...])
-        for n in range(faces // LANES):
-            here = jnp.where(band_lane == by_face[:, n : n + 1], 1.0, 0.0)
-            table[n * LANES : (n + 1) * LANES, :] = here.astype(jnp.bfloat16)
+
+        def mark(h):
+            tiles = half // LANES
+            for n in range(h * tiles, (h + 1) * tiles):
+                here = jnp.where(band_lane == by_face[:, n : n + 1], 1.0, 0.0)
+                table[n * LANES : (n + 1) * LANES, :] = here.astype(jnp.bfloat16)
+
+        mark(0)
         got_area.wait()
         got_faces.wait()
         weigh(own, 0, 0, face_groups)
@@ -258,6 +263,8 @@
             cut = slice(h * half, (h + 1) * half)
             both = jnp.dot(split(weighted[:, cut]), table[cut, :], preferred_element_type=jnp.float32)
             sums.append(both[0:24] + both[24:48])
+            if h == 0:
+                mark(1)
         for p in range(PLANES):
             here = sums[0] * on_plane[0][p] + sums[1] * on_plane[1][p]
             for q in range(4):

time: 21.8 us -> 21.8 us (level)
  no operation moved by 1% of the time
where the time goes in v7:
time: 21.8 us; the launch traced here: 21.5 us
  Pallas kernels  19.9 us (91%)
  local copies, waits for them, and re-layouts  0.87 us (4%)
  between operations  0.66 us (3%)
    pallas_call x1, Pallas kernels, shards(): pl.pallas_call(kernel, out_shape=pltpu.VMEM((NV, groups, 8, LANES), f32),...  19.9 us
    unnamed x1, local copies, waits for them, and re-layouts  0.87 us

profile of v7, /device:TPU:0, one launch (start us, length us, event | category | flops | bytes accessed | tf_op | source)
XLA Modules:
  0.0 21.5 jit_solution(9216802686539249690)
XLA Ops:
  0.7 19.9 %shard_map.64 = f32[5,36,8,128]{3,2,1,0:T(8,128)S(1)} custom-call(f32[5,36,8,128]{3,2,1,0:T(8,128)} %bitcast.24, bf16[5,5,18,16,128]{4,3,2,1,0:T(8,128)(2,1)} %bitcast.23, f32[5,36,8,128]{3,2,1,0:T(8,128)} %bitcast.25, f32[32,128]{1,0:T(8,128)} %bitcast.26, s32[32,128]{1,0:T(8,128)} %bitcast.27, s32[1]{0:T(128)S(6)} %copy.13.owner), custom_call_target="tpu_custom_call" | custom-call | tf_op jit(solution)/shard_map/pallas_call | solution.py:453
  20.6 0.9 %copy.12 = f32[2,5,18432]{2,0,1:T(2,128)} copy(f32[2,5,18432]{2,0,1:T(2,128)S(1)} %bitcast.22) | data formatting | bytes 1474560

commit v8 on v6

--- a/solution.py
+++ b/solution.py
@@ -204,6 +204,9 @@
         for r in range(1, 4):
             bands = jnp.where(block_row < 2 * r, bands, band_v[pl.ds(4 * g + r, 1), :])
         index[g] = bands
+        here = face_start + g
+        for v in range(NV):
+            result[v, here] += own[v, here] * (pseudo_step * coupling_gain)
 
     row = owner[0]
     planes = (jnp.maximum(row - 1, 0), jnp.minimum(row, PLANES - 1))
@@ -389,7 +392,7 @@
                     jnp.take_along_axis(by_row[v][:, :LANES], lane, axis=1, mode="promise_in_bounds"),
                     jnp.take_along_axis(by_row[v][:, LANES:], lane, axis=1, mode="promise_in_bounds"),
                 )
-                result[v, here] += own[v, here] * (pseudo_step * coupling_gain) - face_mean
+                result[v, here] -= face_mean
 
         each(0, face_groups // 2, mix)
 

time: 21.8 us -> 21.7 us (level)
  no operation moved by 1% of the time
where the time goes in v8:
time: 21.7 us; the launch traced here: 21.5 us
  Pallas kernels  19.9 us (92%)
  local copies, waits for them, and re-layouts  0.87 us (4%)
  between operations  0.66 us (3%)
    pallas_call x1, Pallas kernels, shards(): pl.pallas_call(kernel, out_shape=pltpu.VMEM((NV, groups, 8, LANES), f32),...  19.9 us
    unnamed x1, local copies, waits for them, and re-layouts  0.87 us

profile of v8, /device:TPU:0, one launch (start us, length us, event | category | flops | bytes accessed | tf_op | source)
XLA Modules:
  0.0 21.5 jit_solution(691331627308800712)
XLA Ops:
  0.7 19.9 %shard_map.64 = f32[5,36,8,128]{3,2,1,0:T(8,128)S(1)} custom-call(f32[5,36,8,128]{3,2,1,0:T(8,128)} %bitcast.24, bf16[5,5,18,16,128]{4,3,2,1,0:T(8,128)(2,1)} %bitcast.23, f32[5,36,8,128]{3,2,1,0:T(8,128)} %bitcast.25, f32[32,128]{1,0:T(8,128)} %bitcast.26, s32[32,128]{1,0:T(8,128)} %bitcast.27, s32[1]{0:T(128)S(6)} %copy.13.owner), custom_call_target="tpu_custom_call" | custom-call | tf_op jit(solution)/shard_map/pallas_call | solution.py:449
  20.6 0.9 %copy.12 = f32[2,5,18432]{2,0,1:T(2,128)} copy(f32[2,5,18432]{2,0,1:T(2,128)S(1)} %bitcast.22) | data formatting | bytes 1474560
